TPU v7x, 32 devices: a whole 2x2x4 slice. The times are simulated.
32 devices in a mesh: member: 2 (over y), lon: 16 (over z, x, core).
Axes of the slice: x: 2, y: 2, z: 4, core: 2. Of those that a mesh axis runs over, the one named last changes fastest.
Arguments:
- state_start: float32 [190, 256, 128], P('member', 'lon'), parts along dimension 0, may hold values from -6 to 6
- lift_weight: bfloat16 [95, 256], replicated, may hold values from -0.625 to 0.625
- conv_kernel: float32 [49, 256], replicated, may hold values from -0.875 to 0.875
- norm_gain: float32 [256], replicated, may hold values from 0.1 to 1.9
- up_weight: bfloat16 [256, 1024], replicated, may hold values from -0.375 to 0.375
- down_weight: bfloat16 [1024, 256], replicated, may hold values from -0.1875 to 0.1875
- out_weight: bfloat16 [256, 95], replicated, may hold values from -0.375 to 0.375
- obs_cells: int32 [4, 256, 32, 4], P('member', 'lon'), parts along dimension 0, may hold values from 0 to 127
- obs_weights: float32 [4, 256, 32, 4], P('member', 'lon'), parts along dimension 0, may hold values from 0.1 to 1
- tile_counts: int32 [4, 256], P('member', 'lon'), parts along dimension 0, may hold values from 1 to 32, as said below
- obs_owner: int32 [4, 8192, 1], P('member', 'lon'), parts along dimension 0, may hold values from 0 to 15; in each aligned block of 512 rows (0 to 511, 512 to 1023, ..., all dimensions but the last counted through in order) at most 64 rows name the same one
- obs_values: float32 [4, 16, 16, 64, 95], P('member', 'lon'), parts along dimension 0, may hold values from -6 to 6
- obs_precision: float32 [4, 16, 16, 64, 95], P('member', 'lon'), parts along dimension 0, may hold values from 0.5 to 2
Outputs:
- gradient: float32 [190, 256, 128], P('member', 'lon'), parts along dimension 0
There are 2 independent parts, one for each index of `member`. A program takes and returns all parts, laid end to end along the dimension named above; an argument that names none is the same for every part. Nothing has to cross between parts.
Inputs may be any that keep to these rules, and one draw needn't show every extreme that they name: Slots k >= tile_counts of a tile are padding; some tile of every time holds 32 observations. `obs_owner`: within the 512 slots of one band at one time, no owner is named by more than 64 slots, and some band names one owner exactly 64 times.
All inputs are finite; a program needn't handle non-finite values.
Results may differ from a plain program's by a relative error of at most 0.015.
Values may be sent and summed in bfloat16 or wider, within the bound.
A program may use at most 128 MiB of HBM per device.

v0:
```python
import functools

import jax
import jax.numpy as jnp
from jax import lax
from jax.experimental import pallas as pl
from jax.experimental.pallas import tpu as pltpu
from jax.sharding import PartitionSpec as P

TILE_CELLS = 128


gelu_coef = 0.044715
root_two_pi = 0.7978845608028654
eps_norm = 1e-06
TAPS = 7
REACH = 3
VMEM_LIMIT = 56 * 1024 * 1024


def edges(cells):
    count = lax.axis_size("lon")
    west = lax.ppermute(cells[-REACH:], "lon", [(i, (i + 1) % count) for i in range(count)])
    east = lax.ppermute(cells[:REACH], "lon", [((i + 1) % count, i) for i in range(count)])
    return west, east


def exchange(mid_ref, west_ref, east_ref, send_sem, recv_sem):
    lon_rows = mid_ref.shape[0]
    count = lax.axis_size("lon")
    here = lax.axis_index("lon")
    ahead, behind = lax.rem(here + 1, count), lax.rem(here + count - 1, count)
    barrier = pltpu.get_barrier_semaphore()
    for neighbour in (behind, ahead):
        pl.semaphore_signal(
            barrier,
            inc=1,
            device_id={"lon": neighbour},
            device_id_type=pl.DeviceIdType.MESH,
        )
    pl.semaphore_wait(barrier, 2)
    copies = []
    for at, (source, target, neighbour) in enumerate(
        (
            (mid_ref.at[pl.ds(lon_rows - REACH, REACH)], west_ref, ahead),
            (mid_ref.at[pl.ds(0, REACH)], east_ref, behind),
        )
    ):
        copy = pltpu.make_async_remote_copy(
            src_ref=source,
            dst_ref=target,
            send_sem=send_sem.at[at],
            recv_sem=recv_sem.at[at],
            device_id={"lon": neighbour},
            device_id_type=pl.DeviceIdType.MESH,
        )
        copy.start()
        copies.append(copy)
    return copies


def put_row(pad_ref, row, ref, at):
    lat_cols, hidden = ref.shape[1:]
    zeros = jnp.zeros((8, 128), jnp.float32)
    for h in range(hidden // 128):
        pad_ref[h, row, 0:8, :] = zeros
        pad_ref[h, row, 8 + lat_cols : 16 + lat_cols, :] = zeros
        pad_ref[h, row, 8 : 8 + lat_cols, :] = ref[at, :, h * 128 : (h + 1) * 128].astype(
            jnp.float32
        )


def conv_block(pad_ref, kern_ref, mix_ref, lat_start, wanted, flip):
    halves, lon_pad, _, _ = pad_ref.shape
    last = TAPS * TAPS - 1

    def piece(step, carry):
        h, sub = step // 2, step % 2
        base = pl.multiple_of(lat_start + sub * 8, 8)
        sums = {}
        for j in range(TAPS):
            taps = [i * TAPS + j for i in range(TAPS)]
            weight = [kern_ref[h, last - tap if flip else tap] for tap in taps]
            for row in range(lon_pad):
                users = [(i, row - i) for i in range(TAPS) if row - i in wanted]
                if not users:
                    continue
                cells = pad_ref[h, row, pl.ds(base + j + 8 - REACH, 8), :]
                for i, o in users:
                    term = weight[i] * cells
                    sums[o] = sums[o] + term if o in sums else term
        for o in wanted:
            mix_ref[h, o, pl.ds(pl.multiple_of(sub * 8, 8), 8), :] = sums[o]
        return carry

    lax.fori_loop(0, halves * 2, piece, 0)


def conv_all(mid_ref, kern_ref, pad_ref, mix_ref, west_ref, east_ref, sems, flip, finish):
    lon_rows, lat_cols, _ = mid_ref.shape
    copies = exchange(mid_ref, west_ref, east_ref, *sems) if sems else []
    early = 3 * lat_cols // 64 if sems else 0

    def middle_row(row, carry):
        put_row(pad_ref, row + REACH, mid_ref, row)
        return carry

    lax.fori_loop(0, lon_rows, middle_row, 0)
    inner = tuple(range(REACH, lon_rows - REACH))
    outer = tuple(o for o in range(lon_rows) if o not in inner)
    blocks = lat_cols // 16

    def run(first, end, wanted):
        def block(at, carry):
            lat = pl.multiple_of(at * 16, 16)
            conv_block(pad_ref, kern_ref, mix_ref, lat, wanted, flip)
            for o in wanted:
                halves = [mix_ref[h, o] for h in range(mix_ref.shape[0])]
                finish(o, lat, jnp.concatenate(halves, axis=1))
            return carry

        lax.fori_loop(first, end, block, 0)

    if early:
        run(0, early, inner)
    for copy in copies:
        copy.wait()
    for row in range(REACH):
        put_row(pad_ref, row, west_ref, row)
        put_row(pad_ref, lon_rows + REACH + row, east_ref, row)
    if early:
        run(0, early, outer)
    run(early, blocks, tuple(range(lon_rows)))


def conv_norm_kernel(
    mid_ref,
    kern_ref,
    gain_ref,
    normal_ref,
    normed_ref,
    inverse_ref,
    pad_ref,
    mix_ref,
    west_ref,
    east_ref,
    *sems,
):
    def finish(o, lat, mixed):
        center = mixed - jnp.mean(mixed, axis=1, keepdims=True)
        inverse = lax.rsqrt(jnp.mean(center * center, axis=1, keepdims=True) + eps_norm)
        normal = center * inverse
        normal_ref[o, pl.ds(lat, 16), :] = normal.astype(jnp.bfloat16)
        normed_ref[o, pl.ds(lat, 16), :] = (normal * gain_ref[...]).astype(jnp.bfloat16)
        inverse_ref[o, pl.ds(lat, 16), :] = jnp.broadcast_to(inverse, (16, 128))

    conv_all(mid_ref, kern_ref, pad_ref, mix_ref, west_ref, east_ref, sems, False, finish)


def conv_norm_given_kernel(west_ref, east_ref, *refs):
    conv_norm_kernel(*refs, west_ref, east_ref)


def conv_add_kernel(
    mid_ref, kern_ref, add_ref, out_ref, pad_ref, mix_ref, west_ref, east_ref, *sems
):
    def finish(o, lat, summed):
        total = add_ref[o, pl.ds(lat, 16), :].astype(jnp.float32) + summed
        out_ref[o, pl.ds(lat, 16), :] = total.astype(jnp.bfloat16)

    conv_all(mid_ref, kern_ref, pad_ref, mix_ref, west_ref, east_ref, sems, True, finish)


def conv_scratch(shape):
    lon_rows, lat_cols, hidden = shape
    halves = hidden // 128
    return [
        pltpu.VMEM((halves, lon_rows + 2 * REACH, lat_cols + 16, 128), jnp.float32),
        pltpu.VMEM((halves, lon_rows, 16, 128), jnp.float32),
        pltpu.VMEM((REACH, lat_cols, hidden), jnp.bfloat16),
        pltpu.VMEM((REACH, lat_cols, hidden), jnp.bfloat16),
        pltpu.SemaphoreType.DMA((2,)),
        pltpu.SemaphoreType.DMA((2,)),
    ]


def conv_cost(shape):
    cells = shape[0] * shape[1] * shape[2]
    return pl.CostEstimate(flops=cells * 98, bytes_accessed=cells * 12, transcendentals=0)


def in_vmem(count):
    return [pl.BlockSpec(memory_space=pltpu.VMEM)] * count


def conv_norm(cells, kern, gain, given):
    shape = cells.shape
    return pl.pallas_call(
        conv_norm_given_kernel if given else conv_norm_kernel,
        out_shape=(
            jax.ShapeDtypeStruct(shape, jnp.bfloat16),
            jax.ShapeDtypeStruct(shape, jnp.bfloat16),
            jax.ShapeDtypeStruct(shape[:2] + (128,), jnp.float32),
        ),
        in_specs=in_vmem(5 if given else 3),
        out_specs=tuple(in_vmem(3)),
        scratch_shapes=conv_scratch(shape)[: 2 if given else None],
        cost_estimate=conv_cost(shape),
        compiler_params=pltpu.CompilerParams(vmem_limit_bytes=VMEM_LIMIT)
        if given
        else pltpu.CompilerParams(
            vmem_limit_bytes=VMEM_LIMIT, collective_id=0, has_side_effects=True
        ),
    )(*(edges(cells) if given else ()), cells, kern, gain)


def conv_add(cells, kern, add):
    shape = cells.shape
    return pl.pallas_call(
        conv_add_kernel,
        out_shape=jax.ShapeDtypeStruct(shape, jnp.bfloat16),
        in_specs=in_vmem(3),
        out_specs=pl.BlockSpec(memory_space=pltpu.VMEM),
        scratch_shapes=conv_scratch(shape),
        cost_estimate=conv_cost(shape),
        compiler_params=pltpu.CompilerParams(
            vmem_limit_bytes=VMEM_LIMIT, collective_id=1, has_side_effects=True
        ),
    )(cells, kern, add)


def mlp_kernel(piece, normed_ref, lifted_ref, up_ref, down_ref, block_ref, slope_ref):
    normed = normed_ref[...]
    total = lifted_ref[...].astype(jnp.float32)
    for start in range(0, up_ref.shape[1], piece):
        z = jnp.dot(normed, up_ref[:, start : start + piece], preferred_element_type=jnp.float32)
        square = z * z
        tanh_val = jnp.tanh(z * (root_two_pi + root_two_pi * gelu_coef * square))
        half = 0.5 + 0.5 * tanh_val
        active = (z * half).astype(jnp.bfloat16)
        rest = (1.0 - half).astype(jnp.bfloat16)
        share, arg = half.astype(jnp.bfloat16), z.astype(jnp.bfloat16)
        steep = jnp.bfloat16(6.0 * root_two_pi * gelu_coef)
        bend = arg * (jnp.bfloat16(2.0 * root_two_pi) + steep * (arg * arg))
        slope_ref[:, start : start + piece] = share + share * (rest * bend)
        total = total + jnp.dot(
            active, down_ref[start : start + piece, :], preferred_element_type=jnp.float32
        )
    block_ref[...] = total.astype(jnp.bfloat16)


def mlp(normed, lifted, up_weight, down_weight, rows=512, piece=256):
    amount, hidden = normed.shape
    wide = up_weight.shape[1]
    by_rows = lambda width: pl.BlockSpec((rows, width), lambda r: (r, 0))
    whole = lambda shape: pl.BlockSpec(shape, lambda r: (0, 0))
    return pl.pallas_call(
        functools.partial(mlp_kernel, piece),
        grid=(amount // rows,),
        out_shape=(
            jax.ShapeDtypeStruct((amount, hidden), jnp.bfloat16),
            jax.ShapeDtypeStruct((amount, wide), jnp.bfloat16),
        ),
        in_specs=[by_rows(hidden), by_rows(hidden), whole((hidden, wide)), whole((wide, hidden))],
        out_specs=(by_rows(hidden), by_rows(wide)),
        cost_estimate=pl.CostEstimate(
            flops=4 * amount * hidden * wide,
            bytes_accessed=amount * (wide + 3 * hidden) * 2,
            transcendentals=amount * wide,
        ),
        compiler_params=pltpu.CompilerParams(vmem_limit_bytes=VMEM_LIMIT),
    )(normed, lifted, up_weight, down_weight)


def mlp_back_kernel(
    piece, block_ref, slope_ref, normal_ref, inverse_ref, gain_ref, up_ref, down_ref, out_ref
):
    g_block = block_ref[...]
    across = (((1,), (1,)), ((), ()))
    total = None
    for start in range(0, up_ref.shape[1], piece):
        g_active = lax.dot_general(
            g_block,
            down_ref[start : start + piece, :],
            across,
            preferred_element_type=jnp.float32,
        )
        g_middle = g_active * slope_ref[:, start : start + piece].astype(jnp.float32)
        term = lax.dot_general(
            g_middle.astype(jnp.bfloat16),
            up_ref[:, start : start + piece],
            across,
            preferred_element_type=jnp.float32,
        )
        total = term if total is None else total + term
    g_scaled = total * gain_ref[...]
    normal = normal_ref[...].astype(jnp.float32)
    g_mixed = inverse_ref[:, 0:1] * (
        g_scaled
        - jnp.mean(g_scaled, axis=1, keepdims=True)
        - normal * jnp.mean(g_scaled * normal, axis=1, keepdims=True)
    )
    out_ref[...] = g_mixed.astype(jnp.bfloat16)


def mlp_back(g_block, slope, normal, inverse, gain, up_weight, down_weight, rows=512, piece=256):
    amount, hidden = g_block.shape
    wide = up_weight.shape[1]
    by_rows = lambda width: pl.BlockSpec((rows, width), lambda r: (r, 0))
    whole = lambda shape: pl.BlockSpec(shape, lambda r: (0, 0))
    return pl.pallas_call(
        functools.partial(mlp_back_kernel, piece),
        grid=(amount // rows,),
        out_shape=jax.ShapeDtypeStruct((amount, hidden), jnp.bfloat16),
        in_specs=[
            by_rows(hidden),
            by_rows(wide),
            by_rows(hidden),
            by_rows(128),
            whole((1, hidden)),
            whole((hidden, wide)),
            whole((wide, hidden)),
        ],
        out_specs=by_rows(hidden),
        cost_estimate=pl.CostEstimate(
            flops=4 * amount * hidden * wide,
            bytes_accessed=amount * (2 * wide + 8 * hidden),
            transcendentals=0,
        ),
        compiler_params=pltpu.CompilerParams(vmem_limit_bytes=VMEM_LIMIT),
    )(g_block, slope, normal, inverse, gain, up_weight, down_weight)


def forward_step(state_field, weights, given):
    lift_weight, kern, gain, up_weight, down_weight, out_weight = weights
    channels, lon_rows, lat_cols = state_field.shape
    hidden = lift_weight.shape[1]
    lifted = lax.dot_general(
        state_field.astype(jnp.bfloat16),
        lift_weight,
        (((0,), (0,)), ((), ())),
        preferred_element_type=jnp.float32,
    ).astype(jnp.bfloat16)
    normal, normed, inverse = conv_norm(lifted, kern, gain, given)
    block_out, slope = mlp(
        normed.reshape(-1, hidden), lifted.reshape(-1, hidden), up_weight, down_weight
    )
    change = lax.dot_general(
        out_weight, block_out, (((0,), (1,)), ((), ())), preferred_element_type=jnp.float32
    )
    saved = (normal.reshape(-1, hidden), inverse.reshape(-1, 128), slope)
    return state_field + change.reshape(channels, lon_rows, lat_cols), saved


def backward_step(cotangent, saved, weights):
    lift_weight, kern, gain, up_weight, down_weight, out_weight = weights
    normal, inverse, slope = saved
    channels, lon_rows, lat_cols = cotangent.shape
    hidden = lift_weight.shape[1]
    g_block = lax.dot_general(
        cotangent.astype(jnp.bfloat16),
        out_weight,
        (((0,), (1,)), ((), ())),
        preferred_element_type=jnp.float32,
    ).astype(jnp.bfloat16)
    g_mixed = mlp_back(
        g_block.reshape(-1, hidden), slope, normal, inverse, gain, up_weight, down_weight
    ).reshape(lon_rows, lat_cols, hidden)
    g_lifted = conv_add(g_mixed, kern, g_block)
    g_state = lax.dot_general(
        lift_weight, g_lifted, (((1,), (2,)), ((), ())), preferred_element_type=jnp.float32
    )
    return cotangent + g_state


def tile_ops(cell_ids, point_weights):
    positions = jnp.arange(TILE_CELLS, dtype=jnp.int32)
    return jnp.sum(
        point_weights[..., None] * (cell_ids[..., None] == positions).astype(jnp.float32), axis=2
    )


def to_tiles(state_field):
    channels, lon_rows, lat_cols = state_field.shape
    tile_rows = TILE_CELLS // lon_rows
    split = state_field.reshape(channels, lon_rows, lat_cols // tile_rows, tile_rows)
    return split.transpose(2, 0, 1, 3).reshape(lat_cols // tile_rows, channels, TILE_CELLS)


def from_tiles(tile_sums, lon_rows):
    tile_total, channels, _ = tile_sums.shape
    tile_rows = TILE_CELLS // lon_rows
    split = tile_sums.reshape(tile_total, channels, lon_rows, tile_rows)
    return split.transpose(1, 2, 0, 3).reshape(channels, lon_rows, tile_total * tile_rows)


def slot_selector(owner_ids, band_count, place_count):
    hit = owner_ids[:, None] == jnp.arange(band_count, dtype=jnp.int32)[None, :]
    slots = jnp.arange(owner_ids.shape[0], dtype=jnp.int32)
    earlier = (slots[None, :] < slots[:, None]).astype(jnp.bfloat16)
    before = jnp.dot(earlier, hit.astype(jnp.bfloat16), preferred_element_type=jnp.float32)
    place = jnp.sum(jnp.where(hit, before, 0.0), axis=1).astype(jnp.int32)
    slot_code = owner_ids * place_count + place
    return (
        slot_code[:, None] == jnp.arange(band_count * place_count, dtype=jnp.int32)[None, :]
    ).astype(jnp.bfloat16)


def owners_data(obs_values, obs_precision):
    channels = obs_values.shape[-1]
    widen = ((0, 0), (0, 0), (0, 0), (0, 128 - channels))
    both = jnp.concatenate(
        [jnp.pad(part[:, 0].astype(jnp.bfloat16), widen) for part in (obs_values, obs_precision)],
        axis=3,
    ).transpose(1, 0, 2, 3)
    return lax.all_to_all(both, "lon", split_axis=0, concat_axis=0, tiled=True)


def shards(
    state_start,
    lift_weight,
    conv_kernel,
    norm_gain,
    up_weight,
    down_weight,
    out_weight,
    obs_cells,
    obs_weights,
    tile_counts,
    obs_owner,
    obs_values,
    obs_precision,
):
    hidden = norm_gain.shape[0]
    by_half = lambda taps: jnp.broadcast_to(
        taps.reshape(-1, 1, hidden // 128, 128).transpose(2, 0, 1, 3),
        (hidden // 128, taps.shape[0], 8, 128),
    )
    weights = (
        lift_weight,
        by_half(conv_kernel),
        norm_gain.reshape(1, hidden),
        up_weight,
        down_weight,
        out_weight,
    )
    channels, lon_rows = (state_start.shape[0], state_start.shape[1])
    band_count, place_count = (obs_values.shape[2], obs_values.shape[3])
    tile_total, slot_total = (obs_cells.shape[1], obs_cells.shape[2])
    arrived = owners_data(obs_values, obs_precision)
    operators = [
        tile_ops(obs_cells[moment], obs_weights[moment]).astype(jnp.bfloat16) for moment in range(2)
    ]
    state_one, saved_zero = forward_step(state_start, weights, True)
    state_two, saved_one = forward_step(state_one, weights, False)

    def pulled(moment, state_field):
        selector = slot_selector(obs_owner[moment, :, 0], band_count, place_count)
        chosen = jnp.dot(
            selector,
            arrived[:, moment].reshape(band_count * place_count, -1),
            preferred_element_type=jnp.float32,
        )
        live_slots = (
            (jnp.arange(slot_total, dtype=jnp.int32)[None, :] < tile_counts[moment][:, None])
            .astype(jnp.float32)
            .reshape(-1, 1)
        )
        model_equiv = jnp.einsum(
            "gkc,gsc->gks",
            operators[moment],
            to_tiles(state_field.astype(jnp.bfloat16)),
            preferred_element_type=jnp.float32,
        ).reshape(-1, channels)
        misfit = live_slots * (
            chosen[:, 128 : 128 + channels] * (model_equiv - chosen[:, :channels])
        )
        tile_sums = jnp.einsum(
            "gkc,gks->gsc",
            operators[moment],
            misfit.reshape(tile_total, slot_total, channels).astype(jnp.bfloat16),
            preferred_element_type=jnp.float32,
        )
        return from_tiles(tile_sums, lon_rows)

    carried = backward_step(pulled(1, state_two), saved_one, weights) + pulled(0, state_one)
    return backward_step(carried, saved_zero, weights)


def solution(mesh):
    placed = (
        P("member", "lon", None),
        P(),
        P(),
        P(),
        P(),
        P(),
        P(),
        P("member", "lon", None, None),
        P("member", "lon", None, None),
        P("member", "lon"),
        P("member", "lon", None),
        P("member", "lon", None, None, None),
        P("member", "lon", None, None, None),
    )
    return jax.shard_map(
        shards, mesh=mesh, in_specs=placed, out_specs=P("member", "lon", None), check_vma=False
    )
```

profile of v0, /device:TPU:0, one launch (start us, length us, event | category | flops | bytes accessed | tf_op | source)
XLA Modules:
  0.0 138.3 jit_solution(746048093873814841)
XLA Ops:
  0.0 1.3 convert_element_type.111
  1.3 1.3 convolution_convert_fusion.3.refs_0_
  3.2 5.0 %collective-permute-start.1 = (bf16[3,128,256]{2,1,0:T(8,128)(2,1)S(1)}, bf16[3,128,256]{2,1,0:T(8,128)(2,1)S(1)}, u32[]{:S(2)}, u32[]{:S(2)}) collective-permute-start(bf16[3,128,256]{2,1,0:T(8,128)(2,1)S(1)} %get-tuple-element.27), channel_id=1, source_target_pairs={{1,0},{2,1},{3,2},{4,3},{5,4},{6,5},{7,6},{8,7},{9,8},{10,9},{11,1... | collective-permute-start | bytes 589832 | tf_op jit(solution)/shard_map/ppermute | solution.py:24
  9.7 3.7 %all-to-all-start = ((bf16[16,2,64,256]{3,2,1,0:T(8,128)(2,1)}), bf16[16,2,64,256]{3,2,1,0:T(8,128)(2,1)S(1)}, u32[]{:S(2)}, u32[]{:S(2)}) async-start(bf16[16,2,64,256]{3,2,1,0:T(8,128)(2,1)} %fusion.10), calls=%async_computation | async-start | bytes 2097152 | tf_op jit(solution)/shard_map/all_to_all | solution.py:416
  14.4 1.4 %select_reduce_fusion = (bf16[16,32,128]{2,1,0:T(8,128)(2,1)S(1)}, bf16[16,32,128]{2,1,0:T(8,128)(2,1)S(1)}) fusion(f32[16,32,4]{1,2,0:T(4,128)S(1)} %get-tuple-element.32, s32[16,32,4]{1,2,0:T(4,128)S(1)} %get-tuple-element.30, f32[16,32,4]{1,2,0:T(4,128)S(1)} %get-tuple-element.31, s32[16,32,4]{1,2,0:T(4,128)S(1)} %get-tuple-element.29), kind=kLoop, calls=%fused_computation.29 | loop fusion | flops 1441792 | bytes 294912 | tf_op jit(solution)/shard_map/reduce_sum | solution.py:378
  16.7 14.7 %shard_map.127 = (bf16[16,128,256]{2,1,0:T(8,128)(2,1)}, bf16[16,128,256]{2,1,0:T(8,128)(2,1)}, f32[16,128,128]{2,1,0:T(8,128)}) custom-call(bf16[3,128,256]{2,1,0:T(8,128)(2,1)} %copy-done.7, bf16[3,128,256]{2,1,0:T(8,128)(2,1)} %copy-done.8, bf16[16,128,256]{2,1,0:T(8,128)(2,1)} %copy-done.2, f32[2,49,8,128]{3,2,1,0:T(8,128)} %broadcast_in_dim.11.refs_1_.kern_ref, ...), custom_call_target="tpu_custom_call" | custom-call | flops 51380224 | bytes 6291456 | tf_op jit(solution)/shard_map/pallas_call | solution.py:198
  31.4 7.8 %shard_map.128 = (bf16[2048,256]{1,0:T(8,128)(2,1)}, bf16[2048,1024]{1,0:T(8,128)(2,1)}) custom-call(bf16[2048,256]{1,0:T(8,128)(2,1)} %bitcast.158, bf16[2048,256]{1,0:T(8,128)(2,1)} %bitcast.130, bf16[256,1024]{1,0:T(8,128)(2,1)} %up_ref.7, bf16[1024,256]{1,0:T(8,128)(2,1)} %down_ref.7), custom_call_target="tpu_custom_call" | custom-call | flops 2147483648 | bytes 7340032 | tf_op jit(solution)/shard_map/pallas_call | solution.py:257
  39.2 1.7 %fusion.49 = f32[2048,95]{0,1:T(8,128)S(1)} fusion(bf16[2048,256]{1,0:T(8,128)(2,1)} %get-tuple-element.16, bf16[256,95]{0,1:T(8,128)(2,1)S(1)} %copy-done), kind=kOutput, calls=%fused_computation.89 | convolution fusion | flops 99614720 | bytes 1875456 | tf_op jit(solution)/shard_map/dot_general | solution.py:348
  41.9 1.4 %copy.124 = bf16[95,16,128]{0,2,1:T(8,128)(2,1)S(1)} copy(bf16[95,16,128]{2,1,0:T(8,128)(2,1)} %fusion.25) | data formatting | bytes 778240 | tf_op jit(solution)/shard_map/convert_element_type | solution.py:339
  43.3 1.4 convolution_convert_fusion.2.mid_ref
  44.7 20.7 %shard_map.129 = (bf16[16,128,256]{2,1,0:T(8,128)(2,1)}, bf16[16,128,256]{2,1,0:T(8,128)(2,1)}, f32[16,128,128]{2,1,0:T(8,128)}) custom-call(bf16[16,128,256]{2,1,0:T(8,128)(2,1)} %convolution_convert_fusion.2.mid_ref, f32[2,49,8,128]{3,2,1,0:T(8,128)} %broadcast_in_dim.11.refs_1_.kern_ref, f32[1,256]{1,0:T(1,128)} %bitcast.151), custom_call_target="tpu_custom_call" | custom-call | flops 51380224 | bytes 6291456 | tf_op jit(solution)/shard_map/pallas_call | solution.py:198
  65.4 7.8 %shard_map.130 = (bf16[2048,256]{1,0:T(8,128)(2,1)}, bf16[2048,1024]{1,0:T(8,128)(2,1)}) custom-call(bf16[2048,256]{1,0:T(8,128)(2,1)} %bitcast.159, bf16[2048,256]{1,0:T(8,128)(2,1)} %bitcast.135, bf16[256,1024]{1,0:T(8,128)(2,1)} %up_ref.7, bf16[1024,256]{1,0:T(8,128)(2,1)} %down_ref.7), custom_call_target="tpu_custom_call" | custom-call | flops 2147483648 | bytes 7340032 | tf_op jit(solution)/shard_map/pallas_call | solution.py:257
  73.2 1.7 %fusion.50 = f32[2048,95]{0,1:T(8,128)S(1)} fusion(bf16[2048,256]{1,0:T(8,128)(2,1)} %get-tuple-element.18, bf16[256,95]{0,1:T(8,128)(2,1)S(1)} %copy-done), kind=kOutput, calls=%fused_computation.90 | convolution fusion | flops 99614720 | bytes 1875456 | tf_op jit(solution)/shard_map/dot_general | solution.py:348
  76.0 1.4 %copy.115 = bf16[95,16,128]{0,2,1:T(8,128)(2,1)S(1)} copy(bf16[95,16,128]{2,1,0:T(8,128)(2,1)} %fusion.13) | data formatting | bytes 778240 | tf_op jit(solution)/shard_map/convert_element_type | solution.py:472
  79.5 1.4 %convolution_convert_fusion.1.add_ref = bf16[16,128,256]{2,1,0:T(8,128)(2,1)} fusion(bf16[256,95]{0,1:T(8,128)(2,1)S(1)} %copy-done, f32[95,16,16,8]{0,3,1,2:T(8,128)S(1)} %convolution_bitcast_fusion.1), kind=kOutput, calls=%fused_computation.9 | convolution fusion | flops 100139008 | bytes 1875456 | tf_op jit(solution)/shard_map/dot_general | solution.py:360
  81.0 7.8 %shard_map.131 = bf16[2048,256]{1,0:T(8,128)(2,1)} custom-call(bf16[2048,256]{1,0:T(8,128)(2,1)} %bitcast.127, bf16[2048,1024]{1,0:T(8,128)(2,1)} %get-tuple-element.19.slope_ref, bf16[2048,256]{1,0:T(8,128)(2,1)} %bitcast.141, f32[2048,128]{1,0:T(8,128)} %bitcast.142, f32[1,256]{1,0:T(1,128)} %bitcast.152, bf16[256,1024]{1,0:T(8,128)(2,1)} %up_ref.7, ...), custom_call_target="tpu_custom_call" | custom-call | flops 2147483648 | bytes 8388608 | tf_op jit(solution)/shard_map/pallas_call | solution.py:311
  88.8 16.5 %shard_map.132 = bf16[16,128,256]{2,1,0:T(8,128)(2,1)} custom-call(bf16[16,128,256]{2,1,0:T(8,128)(2,1)} %bitcast.132, f32[2,49,8,128]{3,2,1,0:T(8,128)} %broadcast_in_dim.11.refs_1_.kern_ref, bf16[16,128,256]{2,1,0:T(8,128)(2,1)} %convolution_convert_fusion.1.add_ref), custom_call_target="tpu_custom_call" | custom-call | flops 51380224 | bytes 6291456 | tf_op jit(solution)/shard_map/pallas_call | solution.py:219
  107.0 1.3 copy.131
  108.3 1.6 %fusion.5 = f32[95,16,128]{2,0,1:T(8,128)S(1)} fusion(f32[95,16,128]{2,0,1:T(8,128)} %copy.131, f32[95,16,128]{2,0,1:T(8,128)S(1)} %copy.123, bf16[16,128,256]{2,1,0:T(8,128)(2,1)S(1)} %copy-done.3, bf16[95,256]{1,0:T(8,128)(2,1)S(1)} %copy-done.6), kind=kOutput, calls=%fused_computation.17 | convolution fusion | flops 100003840 | bytes 3431936 | tf_op jit(solution)/shard_map/dot_general | solution.py:370
  109.8 1.4 %convolution_convert_fusion.add_ref = bf16[16,128,256]{2,1,0:T(8,128)(2,1)} fusion(f32[95,16,128]{2,0,1:T(8,128)S(1)} %fusion.5, bf16[256,95]{0,1:T(8,128)(2,1)S(1)} %copy-done), kind=kOutput, calls=%fused_computation.8 | convolution fusion | flops 100333568 | bytes 1875456 | tf_op jit(solution)/shard_map/dot_general | solution.py:360
  111.3 7.7 %shard_map.133 = bf16[2048,256]{1,0:T(8,128)(2,1)} custom-call(bf16[2048,256]{1,0:T(8,128)(2,1)} %bitcast.126, bf16[2048,1024]{1,0:T(8,128)(2,1)} %get-tuple-element.22.slope_ref, bf16[2048,256]{1,0:T(8,128)(2,1)} %bitcast.139, f32[2048,128]{1,0:T(8,128)} %bitcast.140, f32[1,256]{1,0:T(1,128)} %bitcast.153, bf16[256,1024]{1,0:T(8,128)(2,1)} %up_ref.7, ...), custom_call_target="tpu_custom_call" | custom-call | flops 2147483648 | bytes 8388608 | tf_op jit(solution)/shard_map/pallas_call | solution.py:311
  119.0 16.3 %shard_map.134 = bf16[16,128,256]{2,1,0:T(8,128)(2,1)} custom-call(bf16[16,128,256]{2,1,0:T(8,128)(2,1)} %bitcast.131, f32[2,49,8,128]{3,2,1,0:T(8,128)} %broadcast_in_dim.11.refs_1_.kern_ref, bf16[16,128,256]{2,1,0:T(8,128)(2,1)} %convolution_convert_fusion.add_ref), custom_call_target="tpu_custom_call" | custom-call | flops 51380224 | bytes 6291456 | tf_op jit(solution)/shard_map/pallas_call | solution.py:219
  135.3 1.7 %fusion.6 = f32[95,16,128]{2,0,1:T(8,128)S(1)} fusion(f32[95,16,128]{2,0,1:T(8,128)S(1)} %fusion.5, bf16[16,128,256]{2,1,0:T(8,128)(2,1)} %shard_map.134, bf16[95,256]{1,0:T(8,128)(2,1)S(1)} %copy-done.6), kind=kOutput, calls=%fused_computation.18 | convolution fusion | flops 99809280 | bytes 2653696 | tf_op jit(solution)/shard_map/dot_general | solution.py:370
  137.0 1.3 copy.132
  (69 shorter events, 9.8 us)
Async XLA Ops:
  0.0 39.2 %copy-start = (bf16[256,95]{0,1:T(8,128)(2,1)S(1)}, bf16[256,95]{0,1:T(8,128)(2,1)}, u32[]{:S(2)}) copy-start(bf16[256,95]{0,1:T(8,128)(2,1)} %param.19) | copy-start | bytes 145924
  0.0 8.2 %copy-start.4 = (f32[2,1,16,64,95]{4,3,2,1,0:T(8,128)S(1)}, f32[2,1,16,64,95]{4,3,2,1,0:T(8,128)}, u32[]{:S(2)}) copy-start(f32[2,1,16,64,95]{4,3,2,1,0:T(8,128)} %param.24) | copy-start | bytes 2334724
  0.0 8.2 %copy-start.5 = (f32[2,1,16,64,95]{4,3,2,1,0:T(8,128)S(1)}, f32[2,1,16,64,95]{4,3,2,1,0:T(8,128)}, u32[]{:S(2)}) copy-start(f32[2,1,16,64,95]{4,3,2,1,0:T(8,128)} %param.25) | copy-start | bytes 2334724
  2.6 7.1 %copy-start.2 = (bf16[16,128,256]{2,1,0:T(8,128)(2,1)}, bf16[16,128,256]{2,1,0:T(8,128)(2,1)S(1)}, u32[]{:S(2)}) copy-start(bf16[16,128,256]{2,1,0:T(8,128)(2,1)S(1)} %convolution_convert_fusion.3.refs_0_) | copy-start | bytes 3145732
  2.7 13.1 %collective-permute-start = (bf16[3,128,256]{2,1,0:T(8,128)(2,1)S(1)}, bf16[3,128,256]{2,1,0:T(8,128)(2,1)S(1)}, u32[]{:S(2)}, u32[]{:S(2)}) collective-permute-start(bf16[3,128,256]{2,1,0:T(8,128)(2,1)S(1)} %get-tuple-element.28), channel_id=1, source_target_pairs={{0,1},{1,2},{2,3},{3,4},{4,5},{5,6},{6,7},{7,8},{8,9},{9,10},{10,1... | collective-permute-start | bytes 589832 | tf_op jit(solution)/shard_map/ppermute | solution.py:23
  3.2 12.7 %collective-permute-start.1 = (bf16[3,128,256]{2,1,0:T(8,128)(2,1)S(1)}, bf16[3,128,256]{2,1,0:T(8,128)(2,1)S(1)}, u32[]{:S(2)}, u32[]{:S(2)}) collective-permute-start(bf16[3,128,256]{2,1,0:T(8,128)(2,1)S(1)} %get-tuple-element.27), channel_id=1, source_target_pairs={{1,0},{2,1},{3,2},{4,3},{5,4},{6,5},{7,6},{8,7},{9,8},{10,9},{11,1... | collective-permute-start | bytes 589832 | tf_op jit(solution)/shard_map/ppermute | solution.py:24
  8.4 5.0 %copy-start.11 = (f32[49,256]{1,0:T(8,128)S(1)}, f32[49,256]{1,0:T(8,128)}, u32[]{:S(2)}) copy-start(f32[49,256]{1,0:T(8,128)} %param.15) | copy-start | bytes 150532
  8.5 5.0 %copy-start.9 = (s32[2,16,32,4]{2,3,1,0:T(4,128)S(1)}, s32[2,16,32,4]{2,3,1,0:T(4,128)}, u32[]{:S(2)}) copy-start(s32[2,16,32,4]{2,3,1,0:T(4,128)} %param.20) | copy-start | bytes 49156
  8.5 5.0 %copy-start.10 = (f32[2,16,32,4]{2,3,1,0:T(4,128)S(1)}, f32[2,16,32,4]{2,3,1,0:T(4,128)}, u32[]{:S(2)}) copy-start(f32[2,16,32,4]{2,3,1,0:T(4,128)} %param.21) | copy-start | bytes 49156
  8.5 5.0 %copy-start.12 = (s32[2,512,1]{1,2,0:T(1,128)S(1)}, s32[2,512,1]{1,2,0:T(1,128)}, u32[]{:S(2)}) copy-start(s32[2,512,1]{1,2,0:T(1,128)} %param.23) | copy-start | bytes 12292
  8.5 5.3 %copy-start.13 = (s32[2,16]{1,0:T(2,128)S(1)}, s32[2,16]{1,0:T(2,128)}, u32[]{:S(2)}) copy-start(s32[2,16]{1,0:T(2,128)} %param.22) | copy-start | bytes 388
  9.7 68.4 %all-to-all-start = ((bf16[16,2,64,256]{3,2,1,0:T(8,128)(2,1)}), bf16[16,2,64,256]{3,2,1,0:T(8,128)(2,1)S(1)}, u32[]{:S(2)}, u32[]{:S(2)}) async-start(bf16[16,2,64,256]{3,2,1,0:T(8,128)(2,1)} %fusion.10), calls=%async_computation | async-start | bytes 2097152 | tf_op jit(solution)/shard_map/all_to_all | solution.py:416
  15.8 0.9 copy-start.7
  15.8 0.9 copy-start.8
  39.2 1.9 %copy-start.1 = (f32[95,16,128]{2,1,0:T(8,128)S(1)}, f32[95,16,128]{2,1,0:T(8,128)}, u32[]{:S(2)}) copy-start(f32[95,16,128]{2,1,0:T(8,128)} %param.13) | copy-start | bytes 2334724
  40.9 2.4 %copy-start.6 = (bf16[95,256]{1,0:T(8,128)(2,1)S(1)}, bf16[95,256]{1,0:T(8,128)(2,1)}, u32[]{:S(2)}) copy-start(bf16[95,256]{1,0:T(8,128)(2,1)} %param.14) | copy-start | bytes 145924
  106.9 1.4 copy-start.3
where the time goes:
time: 139 us; the launch traced here: 138 us
  Pallas kernels  99.1 us (71%)
  matrix products  15.2 us (11%)
  starting transfers between devices  9.19 us (7%)
  local copies, waits for them, and re-layouts  8.33 us (6%)
  other arithmetic  6.02 us (4%)
    pallas_call x2, Pallas kernels, conv_norm(): pl.pallas_call(conv_norm_given_kernel if given else conv_norm_kernel, out...  35.3 us
    pallas_call x2, Pallas kernels, conv_add(): pl.pallas_call(conv_add_kernel, out_shape=jax.ShapeDtypeStruct(shape, jnp...  32.8 us
    pallas_call x2, Pallas kernels, mlp(): pl.pallas_call(functools.partial(mlp_kernel, piece), grid=(amount // rows...  15.5 us
    pallas_call x2, Pallas kernels, mlp_back(): pl.pallas_call(functools.partial(mlp_back_kernel, piece), grid=(amount //...  15.5 us
    ppermute x1, starting transfers between devices, edges(): lax.ppermute(cells[:REACH], 'lon', [((i + 1) % count, i) for i in range(c...  5.02 us
    all_to_all x1, starting transfers between devices, owners_data(): return lax.all_to_all(both, 'lon', split_axis=0, concat_axis=0, tiled=True)  3.65 us
    dot_general x2, matrix products, forward_step(): lax.dot_general(out_weight, block_out, (((0,), (1,)), ((), ())), preferre...  3.41 us
    dot_general x2, matrix products, backward_step(): lax.dot_general(lift_weight, g_lifted, (((1,), (2,)), ((), ())), preferre...  3.25 us
  transfers between devices with their start and end apart: 3, of which 0 were waited for; matrix products, arithmetic and copies ran while one was open for 11% of the time, Pallas kernels for 37%

commit v1 on v0

v1 whole, which is shorter than its diff:
```python
import jax
import jax.numpy as jnp
from jax import lax
from jax.experimental import pallas as pl
from jax.experimental.pallas import tpu as pltpu
from jax.sharding import PartitionSpec as P

gelu_coef = 0.044715
root_two_pi = 0.7978845608028654
eps_norm = 1e-06
TAPS = 7
REACH = 3
BLOCKS = 8
TILE_LAT = 8
LANES = 128
VMEM_LIMIT = 60 * 1024 * 1024
f32, bf16 = jnp.float32, jnp.bfloat16
ACROSS = (((1,), (1,)), ((), ()))
DOWN = (((0,), (0,)), ((), ()))


def send_rows(ref, sems, at):
    send_sem, recv_sem = sems
    rows = ref.shape[0] - 2 * REACH
    count = lax.axis_size("lon")
    here = lax.axis_index("lon")
    ahead, behind = lax.rem(here + 1, count), lax.rem(here + count - 1, count)
    copies = []
    for side, (start, into, target) in enumerate(
        ((rows, 0, ahead), (REACH, rows + REACH, behind))
    ):
        copy = pltpu.make_async_remote_copy(
            src_ref=ref.at[pl.ds(start, REACH)],
            dst_ref=ref.at[pl.ds(into, REACH)],
            send_sem=send_sem.at[2 * at + side],
            recv_sem=recv_sem.at[2 * at + side],
            device_id={"lon": target},
            device_id_type=pl.DeviceIdType.MESH,
        )
        copy.start()
        copies.append(copy)
    return copies


def put_tiles(xp_ref, row, values):
    runs = values.shape[0] // BLOCKS
    tiles = values.reshape(runs, BLOCKS, values.shape[1])
    block = lax.broadcasted_iota(jnp.int32, (REACH, BLOCKS, values.shape[1]), 1)
    xp_ref[row + REACH, REACH : REACH + runs] = tiles.astype(bf16)
    before = pltpu.roll(tiles[runs - REACH :], 1, 1)
    xp_ref[row + REACH, 0:REACH] = jnp.where(block == 0, 0.0, before).astype(bf16)
    after = pltpu.roll(tiles[:REACH], BLOCKS - 1, 1)
    xp_ref[row + REACH, REACH + runs :] = jnp.where(block == BLOCKS - 1, 0.0, after).astype(bf16)


def conv_tiles(xp_ref, kb_ref, o, start, number, flip):
    last = TAPS * TAPS - 1
    totals = [None] * number
    for i in range(TAPS):
        cells = [xp_ref[o + i, start + q] for q in range(number + TAPS - 1)]
        parts = [[] for _ in range(number)]
        for j in range(TAPS):
            tap = i * TAPS + j
            weight = kb_ref[last - tap if flip else tap]
            for q in range(number):
                parts[q].append(weight * cells[q + j])
                if j in (1, 3, 5):
                    top = parts[q].pop()
                    parts[q][-1] = parts[q][-1] + top
                if j == 3:
                    top = parts[q].pop()
                    parts[q][-1] = parts[q][-1] + top
                if j == 6:
                    top = parts[q].pop()
                    parts[q][-1] = parts[q][-1] + top
                    top = parts[q].pop()
                    parts[q][-1] = parts[q][-1] + top
        for q in range(number):
            term = parts[q][0].astype(f32)
            totals[q] = term if totals[q] is None else totals[q] + term
    return jnp.concatenate(totals, axis=0)


def whole_kernel(
    state_ref,
    lift_ref,
    kern_ref,
    gain_ref,
    up_ref,
    down_ref,
    outw_ref,
    idx_ref,
    wts_ref,
    code_ref,
    vals_ref,
    prec_ref,
    out_ref,
    tin_ref,
    nat_ref,
    kb_ref,
    xp0_ref,
    xp1_ref,
    xp2_ref,
    xp3_ref,
    one_ref,
    two_ref,
    cot_ref,
    normed_ref,
    normal_ref,
    inverse_ref,
    slope_ref,
    gblk_ref,
    op_ref,
    chosen_ref,
    sb_ref,
    rb_ref,
    send_sem,
    recv_sem,
    obs_send,
    obs_recv,
    own_sem,
):
    count = lax.axis_size("lon")
    here = lax.axis_index("lon")
    lon_rows = xp0_ref.shape[0] - 2 * REACH
    runs = xp0_ref.shape[1] - 2 * REACH
    lat_cols = runs * BLOCKS
    hidden = xp0_ref.shape[3]
    wide = up_ref.shape[1]
    channels = vals_ref.shape[-1]
    cap = sb_ref.shape[1] // 2
    slots = code_ref.shape[1]
    sems = (send_sem, recv_sem)
    group = lon_rows // 4
    rows = group * lat_cols
    barrier = pltpu.get_barrier_semaphore()

    def peer(step):
        return lax.rem(here + step, count)

    def greet(step, carry):
        pl.semaphore_signal(
            barrier, inc=1, device_id={"lon": peer(step)}, device_id_type=pl.DeviceIdType.MESH
        )
        return carry

    lax.fori_loop(1, count, greet, 0)

    tin_ref[...] = jnp.zeros_like(tin_ref)

    def tap_row(tap, carry):
        row = kern_ref[pl.ds(tap, 1), :]
        kb_ref[tap] = jnp.broadcast_to(row, (BLOCKS, hidden)).astype(bf16)
        return carry

    lax.fori_loop(0, TAPS * TAPS, tap_row, 0)

    def enter(o, carry):
        tin_ref[0:channels, :] = state_ref[pl.ds(o, channels, stride=lon_rows), :]
        nat_ref[...] = tin_ref[...].T
        base = pl.multiple_of(o * lat_cols, lat_cols)
        cells = jnp.concatenate(
            [nat_ref[pl.ds(r, BLOCKS, stride=runs), :] for r in range(runs)], axis=0
        )
        one_ref[pl.ds(base, lat_cols), :] = cells
        lifted = jnp.dot(cells.astype(bf16), lift_ref[...], preferred_element_type=f32)
        put_tiles(xp0_ref, o, lifted)
        return carry

    lax.fori_loop(0, lon_rows, enter, 0)

    def obs_row(band, carry):
        for moment in range(2):
            at = pl.ds(moment * cap, cap)
            for side, ref in enumerate((vals_ref, prec_ref)):
                padded = jnp.concatenate(
                    [ref[moment, band], jnp.zeros((cap, LANES - channels), f32)], axis=1
                )
                sb_ref[band, at, side * LANES : (side + 1) * LANES] = padded.astype(bf16)
        return carry

    lax.fori_loop(0, count, obs_row, 0)

    pl.semaphore_wait(barrier, count - 1)
    halo = send_rows(xp0_ref, sems, 0)

    def obs_copy(step):
        return pltpu.make_async_remote_copy(
            src_ref=sb_ref.at[peer(step)],
            dst_ref=rb_ref.at[here],
            send_sem=obs_send.at[step - 1],
            recv_sem=obs_recv.at[step - 1],
            device_id={"lon": peer(step)},
            device_id_type=pl.DeviceIdType.MESH,
        )

    def obs_start(step, carry):
        obs_copy(step).start()
        return carry

    lax.fori_loop(1, count, obs_start, 0)
    own = pltpu.make_async_copy(sb_ref.at[here], rb_ref.at[here], own_sem)
    own.start()

    def obs_wait(step, carry):
        copy = obs_copy(step)
        copy.wait_send()
        pltpu.make_async_remote_copy(
            src_ref=sb_ref.at[peer(count - step)],
            dst_ref=rb_ref.at[peer(count - step)],
            send_sem=obs_send.at[step - 1],
            recv_sem=obs_recv.at[step - 1],
            device_id={"lon": peer(step)},
            device_id_type=pl.DeviceIdType.MESH,
        ).wait_recv()
        return carry

    def span(block):
        return pl.ds(pl.multiple_of(block * rows, rows), rows)


    def convolve(xp_ref, flip, finish, halo):
        number = runs // 2

        def at_row(o):
            for part in range(2):
                mixed = conv_tiles(xp_ref, kb_ref, o, part * number, number, flip)
                base = pl.multiple_of(o * lat_cols + part * number * BLOCKS, BLOCKS * number)
                finish(pl.ds(base, number * BLOCKS), mixed)

        def inner(o, carry):
            at_row(o)
            return carry

        def outer(k, carry):
            at_row(jnp.where(k < REACH, k, lon_rows - 2 * REACH + k))
            return carry

        lax.fori_loop(REACH, lon_rows - REACH, inner, 0)
        for copy in halo:
            copy.wait()
        lax.fori_loop(0, 2 * REACH, outer, 0)

    def edges_first(work, send):
        def first(k, carry):
            work(3 * k)
            return carry

        def second(k, carry):
            work(1 + k)
            return carry

        lax.fori_loop(0, 2, first, 0)
        copies = send()
        lax.fori_loop(0, 2, second, 0)
        return copies


    def forward(step, xp_ref, source_ref, target_ref, next_ref, halo):
        def finish(at, mixed):
            center = mixed - jnp.mean(mixed, axis=1, keepdims=True)
            inverse = lax.rsqrt(jnp.mean(center * center, axis=1, keepdims=True) + eps_norm)
            normal = center * inverse
            normal_ref[step, at, :] = normal.astype(bf16)
            normed_ref[at, :] = (normal * gain_ref[...]).astype(bf16)
            inverse_ref[step, at, :] = jnp.broadcast_to(inverse, (mixed.shape[0], LANES))

        convolve(xp_ref, False, finish, halo)

        def work(block):
            at = span(block)
            normed = normed_ref[at, :]
            lifted = xp_ref[pl.ds(REACH + block * group, group), REACH : REACH + runs]
            total = lifted.reshape(rows, hidden).astype(f32)
            piece = 256
            for start in range(0, wide, piece):
                cut = slice(start, start + piece)
                z = jnp.dot(normed, up_ref[:, cut], preferred_element_type=f32)
                square = z * z
                tanh_val = jnp.tanh(z * (root_two_pi + root_two_pi * gelu_coef * square))
                half = 0.5 + 0.5 * tanh_val
                active = (z * half).astype(bf16)
                rest = (1.0 - half).astype(bf16)
                share, arg = half.astype(bf16), z.astype(bf16)
                steep = bf16(6.0 * root_two_pi * gelu_coef)
                bend = arg * (bf16(2.0 * root_two_pi) + steep * (arg * arg))
                slope_ref[step, at, cut] = share + share * (rest * bend)
                total = total + jnp.dot(active, down_ref[cut, :], preferred_element_type=f32)
            change = jnp.dot(total.astype(bf16), outw_ref[...], preferred_element_type=f32)
            state = source_ref[at, :] + change
            target_ref[at, :] = state
            if next_ref is not None:
                lifted = jnp.dot(state.astype(bf16), lift_ref[...], preferred_element_type=f32)
                for k in range(group):
                    put_tiles(
                        next_ref, block * group + k, lifted[k * lat_cols : (k + 1) * lat_cols]
                    )

        return edges_first(work, lambda: send_rows(next_ref, sems, 1) if step == 0 else [])

    halo = forward(0, xp0_ref, one_ref, one_ref, xp1_ref, halo)
    forward(1, xp1_ref, one_ref, two_ref, None, halo)


    lax.fori_loop(1, count, obs_wait, 0)
    own.wait()

    def observe(moment, state, add):
        cells = lax.broadcasted_iota(jnp.int32, (lon_rows * runs, slots), 0)
        lines = jnp.zeros((lon_rows * runs, slots), f32)
        for p in range(idx_ref.shape[1]):
            hit = idx_ref[moment, p : p + 1, :] == cells
            lines = lines + jnp.where(hit, wts_ref[moment, p : p + 1, :], 0.0)
        op_ref[...] = lines.T.astype(bf16)
        places = count * cap
        code = code_ref[moment]
        select = (lax.broadcasted_iota(jnp.int32, (slots, places), 1) == code).astype(f32)
        data = rb_ref[:, moment * cap : (moment + 1) * cap, :].reshape(places, 2 * LANES)
        chosen_ref[...] = jnp.dot(select.astype(bf16), data, preferred_element_type=f32)
        each = slots // BLOCKS
        for block in range(BLOCKS):
            at = pl.ds(block, lon_rows * runs, stride=BLOCKS)
            mine = slice(block * each, (block + 1) * each)
            op = op_ref[mine, :]
            equiv = jnp.dot(op, state[at, :].astype(bf16), preferred_element_type=f32)
            misfit = chosen_ref[mine, LANES:] * (equiv - chosen_ref[mine, :LANES])
            pulled = lax.dot_general(op, misfit.astype(bf16), DOWN, preferred_element_type=f32)
            cot_ref[at, :] = cot_ref[at, :] + pulled if add else pulled


    def backward(step, xp_ref, target_ref):
        def work(block):
            at = span(block)
            g_block = lax.dot_general(
                cot_ref[at, :].astype(bf16), outw_ref[...], ACROSS, preferred_element_type=f32
            ).astype(bf16)
            gblk_ref[at, :] = g_block
            total = None
            piece = 256
            for start in range(0, wide, piece):
                cut = slice(start, start + piece)
                g_active = lax.dot_general(
                    g_block, down_ref[cut, :], ACROSS, preferred_element_type=f32
                )
                g_middle = g_active * slope_ref[step, at, cut].astype(f32)
                term = lax.dot_general(
                    g_middle.astype(bf16), up_ref[:, cut], ACROSS, preferred_element_type=f32
                )
                total = term if total is None else total + term
            g_scaled = total * gain_ref[...]
            normal = normal_ref[step, at, :].astype(f32)
            g_mixed = inverse_ref[step, at, 0:1] * (
                g_scaled
                - jnp.mean(g_scaled, axis=1, keepdims=True)
                - normal * jnp.mean(g_scaled * normal, axis=1, keepdims=True)
            )
            for k in range(group):
                put_tiles(xp_ref, block * group + k, g_mixed[k * lat_cols : (k + 1) * lat_cols])

        halo = edges_first(work, lambda: send_rows(xp_ref, sems, 3 - step))

        def finish(at, summed):
            g_lifted = (gblk_ref[at, :].astype(f32) + summed).astype(bf16)
            g_state = lax.dot_general(g_lifted, lift_ref[...], ACROSS, preferred_element_type=f32)
            target_ref[at, :] = cot_ref[at, :] + g_state

        convolve(xp_ref, True, finish, halo)

    observe(1, two_ref, False)
    backward(1, xp2_ref, cot_ref)
    observe(0, one_ref, True)
    backward(0, xp3_ref, out_ref)


def shards(
    state_start,
    lift_weight,
    conv_kernel,
    norm_gain,
    up_weight,
    down_weight,
    out_weight,
    obs_cells,
    obs_weights,
    tile_counts,
    obs_owner,
    obs_values,
    obs_precision,
):
    channels, lon_rows, lat_cols = state_start.shape
    hidden, wide = up_weight.shape
    runs = lat_cols // BLOCKS
    count, cap = obs_values.shape[2:4]
    tiles, slot_total, points = obs_cells.shape[1:]
    slots = tiles * slot_total
    amount = lon_rows * lat_cols

    first = (jnp.arange(tiles, dtype=jnp.int32) * TILE_LAT) % runs
    idx = (obs_cells // TILE_LAT) * runs + first[None, :, None, None] + obs_cells % TILE_LAT
    by_point = lambda a: a.transpose(0, 3, 1, 2).reshape(2, points, slots)

    owner = obs_owner[:, :, 0]
    hit = owner[:, :, None] == jnp.arange(count, dtype=jnp.int32)
    at = jnp.arange(slots, dtype=jnp.int32)
    earlier = (at[None, :] < at[:, None]).astype(bf16)
    before = jnp.einsum("qp,tpn->tqn", earlier, hit.astype(bf16), preferred_element_type=f32)
    place = jnp.sum(jnp.where(hit, before, 0.0), axis=2).astype(jnp.int32)
    live = jnp.arange(slot_total, dtype=jnp.int32) < tile_counts[:, :, None]
    code = jnp.where(live.reshape(2, slots), owner * cap + place, -1)[:, :, None]

    vmem = pl.BlockSpec(memory_space=pltpu.VMEM)
    field = (lon_rows + 2 * REACH, runs + 2 * REACH, BLOCKS, hidden)
    result = pl.pallas_call(
        whole_kernel,
        out_shape=jax.ShapeDtypeStruct((amount, LANES), f32),
        in_specs=[vmem] * 12,
        out_specs=vmem,
        scratch_shapes=[
            pltpu.VMEM((LANES, LANES), f32),
            pltpu.VMEM((LANES, LANES), f32),
            pltpu.VMEM((TAPS * TAPS, BLOCKS, hidden), bf16),
            *[pltpu.VMEM(field, bf16)] * 4,
            *[pltpu.VMEM((amount, LANES), f32)] * 3,
            pltpu.VMEM((amount, hidden), bf16),
            pltpu.VMEM((2, amount, hidden), bf16),
            pltpu.VMEM((2, amount, LANES), f32),
            pltpu.VMEM((2, amount, wide), bf16),
            pltpu.VMEM((amount, hidden), bf16),
            pltpu.VMEM((slots, lon_rows * runs), bf16),
            pltpu.VMEM((slots, 2 * LANES), f32),
            pltpu.VMEM((count, 2 * cap, 2 * LANES), bf16),
            pltpu.VMEM((count, 2 * cap, 2 * LANES), bf16),
            pltpu.SemaphoreType.DMA((8,)),
            pltpu.SemaphoreType.DMA((8,)),
            pltpu.SemaphoreType.DMA((count - 1,)),
            pltpu.SemaphoreType.DMA((count - 1,)),
            pltpu.SemaphoreType.DMA,
        ],
        compiler_params=pltpu.CompilerParams(
            vmem_limit_bytes=VMEM_LIMIT, collective_id=0, has_side_effects=True
        ),
    )(
        state_start.reshape(channels * lon_rows, lat_cols),
        jnp.pad(lift_weight, ((0, LANES - channels), (0, 0))),
        conv_kernel,
        norm_gain.reshape(1, hidden),
        up_weight,
        down_weight,
        jnp.pad(out_weight, ((0, 0), (0, LANES - channels))),
        by_point(idx),
        by_point(obs_weights),
        code,
        obs_values[:, 0],
        obs_precision[:, 0],
    )
    split = result.reshape(lon_rows, runs, BLOCKS, LANES)[..., :channels]
    return split.transpose(3, 0, 2, 1).reshape(channels, lon_rows, lat_cols)


def solution(mesh):
    placed = (
        P("member", "lon", None),
        P(),
        P(),
        P(),
        P(),
        P(),
        P(),
        P("member", "lon", None, None),
        P("member", "lon", None, None),
        P("member", "lon"),
        P("member", "lon", None),
        P("member", "lon", None, None, None),
        P("member", "lon", None, None, None),
    )
    return jax.shard_map(
        shards, mesh=mesh, in_specs=placed, out_specs=P("member", "lon", None), check_vma=False
    )
```

time: 139 us -> 86.9 us (0.63)
  the two profiles are of different devices: /device:TPU:0 before, /device:TPU:11 now
where the time goes in v1:
time: 86.9 us; the launch traced here: 86.5 us
  Pallas kernels  76.7 us (88%)
  local copies, waits for them, and re-layouts  8.36 us (10%)
  other arithmetic  1.08 us (1%)
    pallas_call x1, Pallas kernels, shards(): pl.pallas_call(whole_kernel, out_shape=jax.ShapeDtypeStruct((amount, LANE...  76.7 us
    unnamed x15, local copies, waits for them, and re-layouts  3.29 us

profile of v1, /device:TPU:11, one launch (start us, length us, event | category | flops | bytes accessed | tf_op | source)
XLA Modules:
  0.0 86.5 jit_solution(3990274140282664399)
XLA Ops:
  0.0 0.7 copy-done.4
  0.7 0.3 fusion.1
  1.0 0.0 copy-start.5
  1.0 0.1 lt.55
  1.1 0.6 copy-done.5
  1.7 0.1 lt.57
  1.8 0.1 fusion.7
  1.9 0.0 copy-start.2
  1.9 0.7 reshape.85.idx_ref
  2.6 0.1 copy-done.2
  2.7 0.6 pad.8.lift_ref
  3.3 0.2 copy-done.3
  3.5 0.1 copy.29
  3.6 0.0 copy-start.1
  3.6 0.6 pad.9.outw_ref
  4.3 0.2 copy-done.1
  4.5 0.7 reshape.86.wts_ref
  5.2 0.5 lt.63
  5.7 0.2 copy.34
  5.9 0.2 copy.35
  6.2 0.9 %add_select_fusion.code_ref = s32[2,512,1]{2,1,0:T(8,128)} fusion(s32[2,512,1]{2,1,0:T(8,128)S(1)} %copy.34, s32[2,512,1]{2,1,0:T(8,128)S(1)} %copy.35, s32[2,512,1]{2,1,0:T(8,128)S(1)} %lt.63, s32[512]{0:T(512)S(1)} %lt.55), kind=kLoop, calls=%fused_computation.5 | loop fusion | flops 3072 | bytes 18432 | tf_op jit(solution)/shard_map/jit(_where)/select_n | solution.py:409
  7.1 76.7 %shard_map.127 = f32[2048,128]{1,0:T(8,128)} custom-call(f32[1520,128]{1,0:T(8,128)} %bitcast.34, bf16[128,256]{1,0:T(8,128)(2,1)} %pad.8.lift_ref, f32[49,256]{1,0:T(8,128)} %kern_ref.1, f32[1,256]{1,0:T(1,128)} %bitcast.37, bf16[256,1024]{1,0:T(8,128)(2,1)} %up_ref.1, bf16[1024,256]{1,0:T(8,128)(2,1)} %down_ref.1, bf16[256,128]{1,0:T(8,128)(2,1)} %pad.9.outw_ref, ...), custom_call_target="tpu_custom_call" | custom-call | tf_op jit(solution)/shard_map/pallas_call | solution.py:413
  83.8 1.4 %copy.39 = f32[16,16,8,95]{3,1,2,0:T(8,128)S(1)} copy(f32[16,16,8,95]{3,2,1,0:T(8,128)} %bitcast.31) | data formatting | bytes 1556480
  85.2 1.3 %copy.37 = f32[95,16,128]{2,1,0:T(8,128)} copy(f32[95,16,128]{0,2,1:T(8,128)S(1)} %bitcast.30) | data formatting | bytes 1556480 | tf_op jit(solution)/shard_map/reshape | solution.py:457
  (11 shorter events, 0.0 us)
Async XLA Ops:
  0.0 0.7 copy-start.4
  0.7 1.1 %copy-start = (s32[2,16,32,4]{2,3,1,0:T(4,128)S(1)}, s32[2,16,32,4]{2,3,1,0:T(4,128)}, u32[]{:S(2)}) copy-start(s32[2,16,32,4]{2,3,1,0:T(4,128)} %param.20) | copy-start | bytes 49156
  1.0 0.7 copy-start.5
  1.9 0.8 copy-start.2
  2.7 0.8 copy-start.3
  3.6 0.8 copy-start.1

commit v2 on v1

v2 whole, which is shorter than its diff:
```python
import jax
import jax.numpy as jnp
from jax import lax
from jax.experimental import pallas as pl
from jax.experimental.pallas import tpu as pltpu
from jax.sharding import PartitionSpec as P

gelu_coef = 0.044715
root_two_pi = 0.7978845608028654
eps_norm = 1e-06
TAPS = 7
REACH = 3
BLOCKS = 8
TILE_LAT = 8
LANES = 128
VMEM_LIMIT = 60 * 1024 * 1024
f32, bf16 = jnp.float32, jnp.bfloat16
ACROSS = (((1,), (1,)), ((), ()))
DOWN = (((0,), (0,)), ((), ()))


def halo_copies(ref, sems, at):
    send_sem, recv_sem = sems
    rows = ref.shape[0] - 2 * REACH
    runs = pl.ds(REACH, ref.shape[1] - 2 * REACH)
    count = lax.axis_size("lon")
    here = lax.axis_index("lon")
    ahead, behind = lax.rem(here + 1, count), lax.rem(here + count - 1, count)
    return [
        pltpu.make_async_remote_copy(
            src_ref=ref.at[pl.ds(start, REACH), runs],
            dst_ref=ref.at[pl.ds(into, REACH), runs],
            send_sem=send_sem.at[2 * at + side],
            recv_sem=recv_sem.at[2 * at + side],
            device_id={"lon": target},
            device_id_type=pl.DeviceIdType.MESH,
        )
        for side, (start, into, target) in enumerate(
            ((rows, 0, ahead), (REACH, rows + REACH, behind))
        )
    ]


def put_ends(xp_ref, at, low, high):
    block = lax.broadcasted_iota(jnp.int32, low.shape, 1)
    runs = xp_ref.shape[1] - 2 * REACH
    before = pltpu.roll(high, 1, 1)
    xp_ref[at, 0:REACH] = jnp.where(block == 0, 0.0, before).astype(bf16)
    after = pltpu.roll(low, BLOCKS - 1, 1)
    xp_ref[at, REACH + runs :] = jnp.where(block == BLOCKS - 1, 0.0, after).astype(bf16)


def put_tiles(xp_ref, row, values):
    runs = values.shape[0] // BLOCKS
    tiles = values.reshape(runs, BLOCKS, values.shape[1])
    xp_ref[row + REACH, REACH : REACH + runs] = tiles.astype(bf16)
    put_ends(xp_ref, row + REACH, tiles[:REACH], tiles[runs - REACH :])


def tree(terms):
    while len(terms) > 1:
        terms = [
            terms[k] + terms[k + 1] if k + 1 < len(terms) else terms[k]
            for k in range(0, len(terms), 2)
        ]
    return terms[0]


def conv_row(xp_ref, kb_ref, mix_ref, o, flip):
    runs = mix_ref.shape[1]
    last = TAPS * TAPS - 1
    for first in range(0, TAPS, 2):
        lines = range(first, min(first + 2, TAPS))
        weights = {}
        for i in lines:
            for j in range(TAPS):
                tap = i * TAPS + j
                weights[i, j] = kb_ref[last - tap if flip else tap]
        window = {i: [xp_ref[o + i, q] for q in range(TAPS - 1)] for i in lines}
        for r in range(runs):
            sums = []
            for i in lines:
                window[i].append(xp_ref[o + i, r + TAPS - 1])
                sums.append(tree([weights[i, j] * window[i][j] for j in range(TAPS)]))
                window[i].pop(0)
            term = tree(sums).astype(f32)
            mix_ref[o, r] = term if first == 0 else mix_ref[o, r] + term


def whole_kernel(
    state_ref,
    lift_ref,
    kern_ref,
    gain_ref,
    up_ref,
    down_ref,
    outw_ref,
    cell_ref,
    wts_ref,
    limit_ref,
    owner_ref,
    vals_ref,
    prec_ref,
    out_ref,
    tin_ref,
    nat_ref,
    pad_ref,
    liftp_ref,
    outp_ref,
    kb_ref,
    xp0_ref,
    xp1_ref,
    xp2_ref,
    xp3_ref,
    one_ref,
    two_ref,
    cot_ref,
    pull_ref,
    mix_ref,
    normal_ref,
    inverse_ref,
    slope_ref,
    gblk_ref,
    code_ref,
    op_ref,
    chosen_ref,
    sb_ref,
    rb_ref,
    send_sem,
    recv_sem,
    obs_send,
    obs_recv,
    own_sem,
):
    count = lax.axis_size("lon")
    here = lax.axis_index("lon")
    lon_rows, runs, _, hidden = mix_ref.shape
    lat_cols = runs * BLOCKS
    wide = up_ref.shape[1]
    channels = vals_ref.shape[-1]
    cap = vals_ref.shape[2]
    tiles, points, each = cell_ref.shape[1:]
    slots = tiles * each
    sems = (send_sem, recv_sem)
    quarter = lon_rows // 4
    inner = ((quarter, lon_rows - quarter),)
    edges = ((0, quarter), (lon_rows - quarter, lon_rows))
    barrier = pltpu.get_barrier_semaphore()
    ones = jnp.full((hidden, LANES), 1.0 / hidden, bf16)

    def peer(step):
        return lax.rem(here + step, count)

    def greet(step, carry):
        pl.semaphore_signal(
            barrier, inc=1, device_id={"lon": peer(step)}, device_id_type=pl.DeviceIdType.MESH
        )
        return carry

    lax.fori_loop(1, count, greet, 0)


    for ref, into_ref in ((lift_ref, liftp_ref), (outw_ref, outp_ref)):
        pad_ref[...] = jnp.zeros_like(pad_ref)
        pad_ref[0:channels, :] = ref[...].astype(f32)
        into_ref[...] = pad_ref[...].astype(bf16)

    tin_ref[...] = jnp.zeros_like(tin_ref)

    def tap_row(tap, carry):
        row = kern_ref[pl.ds(tap, 1), :]
        kb_ref[tap] = jnp.broadcast_to(row, (BLOCKS, hidden)).astype(bf16)
        return carry

    lax.fori_loop(0, TAPS * TAPS, tap_row, 0)

    def enter(o, carry):
        tin_ref[0:channels, :] = state_ref[pl.ds(o, channels, stride=lon_rows), :]
        nat_ref[...] = tin_ref[...].T
        base = pl.multiple_of(o * lat_cols, lat_cols)
        cells = jnp.concatenate(
            [nat_ref[pl.ds(r, BLOCKS, stride=runs), :] for r in range(runs)], axis=0
        )
        one_ref[pl.ds(base, lat_cols), :] = cells
        lifted = jnp.dot(cells.astype(bf16), liftp_ref[...], preferred_element_type=f32)
        put_tiles(xp0_ref, o, lifted)
        return carry

    lax.fori_loop(0, lon_rows, enter, 0)


    def obs_row(band, carry):
        for moment in range(2):
            for side, ref in enumerate((vals_ref, prec_ref)):
                padded = jnp.concatenate(
                    [ref[moment, band], jnp.zeros((cap, LANES - channels), f32)], axis=1
                )
                sb_ref[moment, band, :, side * LANES : (side + 1) * LANES] = padded.astype(bf16)
        return carry

    lax.fori_loop(0, count, obs_row, 0)


    def lookup(moment):
        owner = owner_ref[moment]
        column = jnp.broadcast_to(owner.astype(f32), (LANES, slots)).T
        pieces = []
        for part in range(slots // LANES):
            row = owner[:, part * LANES : (part + 1) * LANES]
            earlier = lax.broadcasted_iota(jnp.int32, (slots, LANES), 0)
            later = lax.broadcasted_iota(jnp.int32, (slots, LANES), 1) + part * LANES
            same = (column == row.astype(f32)) & (earlier < later)
            place = jnp.sum(jnp.where(same, 1.0, 0.0), axis=0, keepdims=True)
            lane = lax.broadcasted_iota(jnp.int32, (1, LANES), 1)
            limit = jnp.zeros((1, LANES), jnp.int32)
            for k in range(LANES // each):
                tile = part * (LANES // each) + k
                limit = jnp.where(lane >= k * each, limit_ref[moment, tile] + k * each, limit)
            code = row.astype(f32) * cap + place
            pieces.append(jnp.where(lane < limit, code, -1.0))
        code = jnp.concatenate(pieces, axis=1)
        code_ref[moment] = jnp.broadcast_to(code, (LANES, slots)).T

    lookup(0)
    lookup(1)

    pl.semaphore_wait(barrier, count - 1)

    def send(ref, at):
        for copy in halo_copies(ref, sems, at):
            copy.start()

    def arrive(ref, at):
        for copy in halo_copies(ref, sems, at):
            copy.wait()

        def ends(k, carry):
            row = jnp.where(k < REACH, k, lon_rows + k)
            low = ref[row, REACH : 2 * REACH].astype(f32)
            high = ref[row, runs : runs + REACH].astype(f32)
            put_ends(ref, row, low, high)
            return carry

        lax.fori_loop(0, 2 * REACH, ends, 0)

    def obs_copy(moment, step, band):
        return pltpu.make_async_remote_copy(
            src_ref=sb_ref.at[moment, band],
            dst_ref=rb_ref.at[moment, here],
            send_sem=obs_send.at[moment, step - 1],
            recv_sem=obs_recv.at[moment, step - 1],
            device_id={"lon": peer(step)},
            device_id_type=pl.DeviceIdType.MESH,
        )

    def own_copy(moment):
        return pltpu.make_async_copy(
            sb_ref.at[moment, here], rb_ref.at[moment, here], own_sem.at[moment]
        )

    def obs_start(moment):
        def start(step, carry):
            obs_copy(moment, step, peer(step)).start()
            return carry

        lax.fori_loop(1, count, start, 0)
        own_copy(moment).start()

    def obs_wait(moment):
        def wait(step, carry):
            obs_copy(moment, step, peer(step)).wait_send()
            source = peer(count - step)
            pltpu.make_async_remote_copy(
                src_ref=sb_ref.at[moment, source],
                dst_ref=rb_ref.at[moment, source],
                send_sem=obs_send.at[moment, step - 1],
                recv_sem=obs_recv.at[moment, step - 1],
                device_id={"lon": peer(step)},
                device_id_type=pl.DeviceIdType.MESH,
            ).wait_recv()
            return carry

        lax.fori_loop(1, count, wait, 0)
        own_copy(moment).wait()


    def take(load, part):
        chunks = [load(a, b) for a, b in part]
        return chunks[0] if len(chunks) == 1 else jnp.concatenate(chunks, axis=0)

    def cells(ref):
        return lambda a, b: ref[a * lat_cols : b * lat_cols, :]

    def leading(ref, step):
        return lambda a, b: ref[step, a * lat_cols : b * lat_cols, :]

    def put(ref, part, values, step=None):
        at = 0
        for a, b in part:
            size = (b - a) * lat_cols
            where = slice(a * lat_cols, b * lat_cols)
            if step is None:
                ref[where, :] = values[at : at + size]
            else:
                ref[step, where, :] = values[at : at + size]
            at += size

    def put_field(xp_ref, part, values):
        at = 0
        for a, b in part:
            for o in range(a, b):
                put_tiles(xp_ref, o, values[at : at + lat_cols])
                at += lat_cols

    def sums(part):
        return take(
            lambda a, b: mix_ref[a:b].reshape((b - a) * lat_cols, hidden),
            part,
        )

    def mean(values):
        wide_mean = jnp.dot(values.astype(bf16), ones, preferred_element_type=f32)
        return jnp.concatenate([wide_mean] * (hidden // LANES), axis=1)

    def conv_inner(xp_ref, flip):
        def body(o, carry):
            conv_row(xp_ref, kb_ref, mix_ref, o, flip)
            return carry

        lax.fori_loop(REACH, lon_rows - REACH, body, 0)

    def conv_outer(xp_ref, flip):
        def body(k, carry):
            o = jnp.where(k < REACH, k, lon_rows - 2 * REACH + k)
            conv_row(xp_ref, kb_ref, mix_ref, o, flip)
            return carry

        lax.fori_loop(0, 2 * REACH, body, 0)

    def forward(step, part, xp_ref, source_ref, target_ref, next_ref):
        mixed = sums(part)
        center = mixed - mean(mixed)
        inverse = lax.rsqrt(mean(center * center) + eps_norm)
        normal = center * inverse
        put(normal_ref, part, normal.astype(bf16), step)
        put(inverse_ref, part, inverse[:, :LANES], step)
        normed = (normal * gain_ref[...]).astype(bf16)
        total = take(
            lambda a, b: xp_ref[a + REACH : b + REACH, REACH : REACH + runs]
            .reshape((b - a) * lat_cols, hidden)
            .astype(f32),
            part,
        )
        piece = 256
        one = bf16(root_two_pi)
        three = bf16(root_two_pi * gelu_coef)
        half_one = bf16(0.5)
        for start in range(0, wide, piece):
            cut = slice(start, start + piece)
            z = jnp.dot(normed, up_ref[:, cut], preferred_element_type=f32).astype(bf16)
            square = z * z
            tanh_val = jnp.tanh(z * (one + three * square))
            share = half_one + half_one * tanh_val
            active = z * share
            rest = bf16(1.0) - share
            bend = z * (bf16(2.0) * one + bf16(6.0) * three * square)
            slope = share + share * (rest * bend)
            at = 0
            for a, b in part:
                size = (b - a) * lat_cols
                slope_ref[step, a * lat_cols : b * lat_cols, cut] = slope[at : at + size]
                at += size
            total = total + jnp.dot(active, down_ref[cut, :], preferred_element_type=f32)
        change = lax.dot_general(
            total.astype(bf16), outp_ref[...], ACROSS, preferred_element_type=f32
        )
        state = take(cells(source_ref), part) + change
        put(target_ref, part, state)
        if next_ref is not None:
            lifted = jnp.dot(state.astype(bf16), liftp_ref[...], preferred_element_type=f32)
            put_field(next_ref, part, lifted)

    def observe(moment, state_ref, target_ref):
        spots = lon_rows * runs
        by_point = lambda ref: jnp.concatenate([ref[moment, g] for g in range(tiles)], axis=1)
        cell = by_point(cell_ref)
        lane = lax.broadcasted_iota(jnp.int32, (points, slots), 1)
        first = ((lane // each) * TILE_LAT) % runs
        spot = (cell // TILE_LAT) * runs + first + cell % TILE_LAT
        weight = by_point(wts_ref)
        number = lax.broadcasted_iota(jnp.int32, (spots, slots), 0)
        lines = jnp.zeros((spots, slots), f32)
        for p in range(points):
            hit = spot[p : p + 1, :] == number
            lines = lines + jnp.where(hit, weight[p : p + 1, :], 0.0)
        op_ref[...] = lines.T.astype(bf16)
        places = count * cap
        code = code_ref[moment]
        line = lax.broadcasted_iota(jnp.int32, (slots, LANES), 1).astype(f32)
        select = jnp.concatenate(
            [
                jnp.where(line + float(start) == code, 1.0, 0.0).astype(bf16)
                for start in range(0, places, LANES)
            ],
            axis=1,
        )
        data = rb_ref[moment].reshape(places, 2 * LANES)
        chosen_ref[...] = jnp.dot(select, data, preferred_element_type=f32)
        size = slots // BLOCKS
        for block in range(BLOCKS):
            at = pl.ds(block, spots, stride=BLOCKS)
            mine = slice(block * size, (block + 1) * size)
            op = op_ref[mine, :]
            equiv = jnp.dot(op, state_ref[at, :].astype(bf16), preferred_element_type=f32)
            misfit = chosen_ref[mine, LANES:] * (equiv - chosen_ref[mine, :LANES])
            target_ref[at, :] = lax.dot_general(
                op, misfit.astype(bf16), DOWN, preferred_element_type=f32
            )

    def gathered(part):
        g_lifted = (take(cells(gblk_ref), part).astype(f32) + sums(part)).astype(bf16)
        g_state = lax.dot_general(g_lifted, liftp_ref[...], ACROSS, preferred_element_type=f32)
        return take(cells(cot_ref), part) + g_state

    def backward(step, part, xp_ref, cotangent):
        g_block = jnp.dot(cotangent.astype(bf16), outp_ref[...], preferred_element_type=f32)
        g_block = g_block.astype(bf16)
        put(gblk_ref, part, g_block)
        total = None
        piece = 256
        for start in range(0, wide, piece):
            cut = slice(start, start + piece)
            g_active = lax.dot_general(
                g_block, down_ref[cut, :], ACROSS, preferred_element_type=f32
            )
            slope = take(lambda a, b: slope_ref[step, a * lat_cols : b * lat_cols, cut], part)
            term = lax.dot_general(
                g_active.astype(bf16) * slope, up_ref[:, cut], ACROSS, preferred_element_type=f32
            )
            total = term if total is None else total + term
        g_scaled = total * gain_ref[...]
        normal = take(leading(normal_ref, step), part).astype(f32)
        inverse = take(leading(inverse_ref, step), part)
        inverse = jnp.concatenate([inverse] * (hidden // LANES), axis=1)
        g_mixed = inverse * (g_scaled - mean(g_scaled) - normal * mean(g_scaled * normal))
        put_field(xp_ref, part, g_mixed)

    def leave(part):
        put(cot_ref, part, gathered(part))
        for a, b in part:

            def body(o, carry):
                base = o * lat_cols
                rows = [cot_ref[pl.ds(base + k, runs, stride=BLOCKS), :] for k in range(BLOCKS)]
                turned = jnp.concatenate(rows, axis=0).T
                out_ref[pl.ds(o, channels, stride=lon_rows), :] = turned[:channels]
                return carry

            lax.fori_loop(a, b, body, 0)


    send(xp0_ref, 0)
    obs_start(1)
    conv_inner(xp0_ref, False)
    forward(0, inner, xp0_ref, one_ref, one_ref, xp1_ref)
    arrive(xp0_ref, 0)
    conv_outer(xp0_ref, False)
    forward(0, edges, xp0_ref, one_ref, one_ref, xp1_ref)
    send(xp1_ref, 1)
    conv_inner(xp1_ref, False)
    forward(1, inner, xp1_ref, one_ref, two_ref, None)
    arrive(xp1_ref, 1)
    obs_start(0)
    conv_outer(xp1_ref, False)
    forward(1, edges, xp1_ref, one_ref, two_ref, None)
    obs_wait(1)
    observe(1, two_ref, cot_ref)
    backward(1, edges, xp2_ref, take(cells(cot_ref), edges))
    send(xp2_ref, 2)
    backward(1, inner, xp2_ref, take(cells(cot_ref), inner))
    conv_inner(xp2_ref, True)
    obs_wait(0)
    observe(0, one_ref, pull_ref)
    arrive(xp2_ref, 2)
    conv_outer(xp2_ref, True)

    def carried(part):
        value = gathered(part) + take(cells(pull_ref), part)
        put(cot_ref, part, value)
        return value

    backward(0, edges, xp3_ref, carried(edges))
    send(xp3_ref, 3)
    backward(0, inner, xp3_ref, carried(inner))
    conv_inner(xp3_ref, True)
    leave(inner)
    arrive(xp3_ref, 3)
    conv_outer(xp3_ref, True)
    leave(edges)


def shards(
    state_start,
    lift_weight,
    conv_kernel,
    norm_gain,
    up_weight,
    down_weight,
    out_weight,
    obs_cells,
    obs_weights,
    tile_counts,
    obs_owner,
    obs_values,
    obs_precision,
):
    channels, lon_rows, lat_cols = state_start.shape
    hidden, wide = up_weight.shape
    runs = lat_cols // BLOCKS
    count, cap = obs_values.shape[2:4]
    tiles, slot_total = obs_cells.shape[1:3]
    slots = tiles * slot_total
    amount = lon_rows * lat_cols

    vmem = pl.BlockSpec(memory_space=pltpu.VMEM)
    smem = pl.BlockSpec(memory_space=pltpu.SMEM)
    field = (lon_rows + 2 * REACH, runs + 2 * REACH, BLOCKS, hidden)
    result = pl.pallas_call(
        whole_kernel,
        out_shape=jax.ShapeDtypeStruct((channels * lon_rows, lat_cols), f32),
        in_specs=[vmem] * 9 + [smem] + [vmem] * 3,
        out_specs=vmem,
        scratch_shapes=[
            pltpu.VMEM((LANES, LANES), f32),
            pltpu.VMEM((LANES, LANES), f32),
            pltpu.VMEM((LANES, hidden), f32),
            pltpu.VMEM((LANES, hidden), bf16),
            pltpu.VMEM((LANES, hidden), bf16),
            pltpu.VMEM((TAPS * TAPS, BLOCKS, hidden), bf16),
            *[pltpu.VMEM(field, bf16)] * 4,
            *[pltpu.VMEM((amount, LANES), f32)] * 4,
            pltpu.VMEM((lon_rows, runs, BLOCKS, hidden), f32),
            pltpu.VMEM((2, amount, hidden), bf16),
            pltpu.VMEM((2, amount, LANES), f32),
            pltpu.VMEM((2, amount, wide), bf16),
            pltpu.VMEM((amount, hidden), bf16),
            pltpu.VMEM((2, slots, LANES), f32),
            pltpu.VMEM((slots, lon_rows * runs), bf16),
            pltpu.VMEM((slots, 2 * LANES), f32),
            pltpu.VMEM((2, count, cap, 2 * LANES), bf16),
            pltpu.VMEM((2, count, cap, 2 * LANES), bf16),
            pltpu.SemaphoreType.DMA((8,)),
            pltpu.SemaphoreType.DMA((8,)),
            pltpu.SemaphoreType.DMA((2, count - 1)),
            pltpu.SemaphoreType.DMA((2, count - 1)),
            pltpu.SemaphoreType.DMA((2,)),
        ],
        compiler_params=pltpu.CompilerParams(
            vmem_limit_bytes=VMEM_LIMIT, collective_id=0, has_side_effects=True
        ),
    )(
        state_start.reshape(channels * lon_rows, lat_cols),
        lift_weight,
        conv_kernel,
        norm_gain.reshape(1, hidden),
        up_weight,
        down_weight,
        out_weight.T,
        obs_cells.transpose(0, 1, 3, 2),
        obs_weights.transpose(0, 1, 3, 2),
        tile_counts,
        obs_owner.transpose(0, 2, 1),
        obs_values[:, 0],
        obs_precision[:, 0],
    )
    return result.reshape(channels, lon_rows, lat_cols)


def solution(mesh):
    placed = (
        P("member", "lon", None),
        P(),
        P(),
        P(),
        P(),
        P(),
        P(),
        P("member", "lon", None, None),
        P("member", "lon", None, None),
        P("member", "lon"),
        P("member", "lon", None),
        P("member", "lon", None, None, None),
        P("member", "lon", None, None, None),
    )
    return jax.shard_map(
        shards, mesh=mesh, in_specs=placed, out_specs=P("member", "lon", None), check_vma=False
    )
```

time: 86.9 us -> 61.8 us (0.71)
  Pallas kernels: 76.7 us -> 58.6 us
  local copies, waits for them, and re-layouts: 8.36 us -> 2.06 us
  other arithmetic: 1.08 us -> 0 us
    pallas_call x1, Pallas kernels: 76.7 us -> 58.6 us  [shards(): pl.pallas_call(whole_kernel, out_shape=jax.ShapeDtypeStruct((channels * l...]
    reshape x3 -> x0, local copies, waits for them, and re-layouts: 2.68 us -> none  [the longest x2 1.38 us: shards(): by_point = lambda a: a.transpose(0, 3, 1, 2).reshape(2, points, slots)]
    pad x2 -> x0, local copies, waits for them, and re-layouts: 1.26 us -> none  [the longest x1 0.64 us: shards(): jnp.pad(out_weight, ((0, 0), (0, LANES - channels)))]
    unnamed x15 -> x1, local copies, waits for them, and re-layouts: 3.29 us -> 2.06 us
    select_n x2 -> x0, other arithmetic: 0.94 us -> none  [the longest x1 0.93 us: shards(): jnp.where(live.reshape(2, slots), owner * cap + place, -1)[:, :, None]]
where the time goes in v2:
time: 61.8 us; the launch traced here: 60.7 us
  Pallas kernels  58.6 us (95%)
  local copies, waits for them, and re-layouts  2.06 us (3%)
    pallas_call x1, Pallas kernels, shards(): pl.pallas_call(whole_kernel, out_shape=jax.ShapeDtypeStruct((channels * l...  58.6 us
    unnamed x1, local copies, waits for them, and re-layouts  2.06 us

profile of v2, /device:TPU:11, one launch (start us, length us, event | category | flops | bytes accessed | tf_op | source)
XLA Modules:
  0.0 60.7 jit_solution(740267969366670905)
XLA Ops:
  0.0 58.6 %shard_map.127 = f32[1520,128]{1,0:T(8,128)} custom-call(f32[1520,128]{1,0:T(8,128)} %bitcast.12, bf16[95,256]{1,0:T(8,128)(2,1)} %lift_ref.1, f32[49,256]{1,0:T(8,128)} %kern_ref.1, f32[1,256]{1,0:T(1,128)} %bitcast.17, bf16[256,1024]{1,0:T(8,128)(2,1)} %up_ref.1, bf16[1024,256]{1,0:T(8,128)(2,1)} %down_ref.1, bf16[95,256]{1,0:T(8,128)(2,1)} %bitcast.15, ...), custom_call_target="tpu_custom_call" | custom-call | tf_op jit(solution)/shard_map/pallas_call | solution.py:528
  58.6 2.1 %copy.15 = f32[95,16,128]{2,1,0:T(8,128)} copy(f32[95,16,128]{2,1,0:T(8,128)} %bitcast.9) | data formatting | bytes 1556480

commit v3 on v2

--- a/solution.py
+++ b/solution.py
@@ -19,25 +19,21 @@
 DOWN = (((0,), (0,)), ((), ()))
 
 
-def halo_copies(ref, sems, at):
+def edge_copies(out_ref, in_ref, sems, at):
     send_sem, recv_sem = sems
-    rows = ref.shape[0] - 2 * REACH
-    runs = pl.ds(REACH, ref.shape[1] - 2 * REACH)
     count = lax.axis_size("lon")
     here = lax.axis_index("lon")
     ahead, behind = lax.rem(here + 1, count), lax.rem(here + count - 1, count)
     return [
         pltpu.make_async_remote_copy(
-            src_ref=ref.at[pl.ds(start, REACH), runs],
-            dst_ref=ref.at[pl.ds(into, REACH), runs],
+            src_ref=out_ref.at[at, side],
+            dst_ref=in_ref.at[at, 1 - side],
             send_sem=send_sem.at[2 * at + side],
-            recv_sem=recv_sem.at[2 * at + side],
+            recv_sem=recv_sem.at[2 * at + 1 - side],
             device_id={"lon": target},
             device_id_type=pl.DeviceIdType.MESH,
         )
-        for side, (start, into, target) in enumerate(
-            ((rows, 0, ahead), (REACH, rows + REACH, behind))
-        )
+        for side, target in enumerate((behind, ahead))
     ]
 
 
@@ -66,11 +62,11 @@
     return terms[0]
 
 
-def conv_row(xp_ref, kb_ref, mix_ref, o, flip):
+def conv_row(xp_ref, kb_ref, mix_ref, o, to, flip, taps=range(TAPS)):
     runs = mix_ref.shape[1]
     last = TAPS * TAPS - 1
-    for first in range(0, TAPS, 2):
-        lines = range(first, min(first + 2, TAPS))
+    for first in range(0, len(taps), 2):
+        lines = taps[first : first + 2]
         weights = {}
         for i in lines:
             for j in range(TAPS):
@@ -84,7 +80,7 @@
                 sums.append(tree([weights[i, j] * window[i][j] for j in range(TAPS)]))
                 window[i].pop(0)
             term = tree(sums).astype(f32)
-            mix_ref[o, r] = term if first == 0 else mix_ref[o, r] + term
+            mix_ref[to, r] = term if first == 0 else mix_ref[to, r] + term
 
 
 def whole_kernel(
@@ -121,11 +117,16 @@
     inverse_ref,
     slope_ref,
     gblk_ref,
+    land_ref,
+    edge_ref,
+    halo_ref,
     code_ref,
     op_ref,
     chosen_ref,
-    sb_ref,
-    rb_ref,
+    late_ref,
+    early_ref,
+    late_in_ref,
+    early_in_ref,
     send_sem,
     recv_sem,
     obs_send,
@@ -189,13 +190,22 @@
     lax.fori_loop(0, lon_rows, enter, 0)
 
 
+    free = LANES - channels
+    turns = [(channels - (channels - free * (2 - k))) % LANES for k in range(2)] + [channels]
+
     def obs_row(band, carry):
-        for moment in range(2):
-            for side, ref in enumerate((vals_ref, prec_ref)):
-                padded = jnp.concatenate(
-                    [ref[moment, band], jnp.zeros((cap, LANES - channels), f32)], axis=1
-                )
-                sb_ref[moment, band, :, side * LANES : (side + 1) * LANES] = padded.astype(bf16)
+        filled = lambda part: jnp.concatenate(
+            [part, jnp.zeros((cap, LANES - channels), f32)], axis=1
+        )
+        spare = filled(prec_ref[0, band])
+        lane = lax.broadcasted_iota(jnp.int32, (cap, LANES), 1)
+        for place, part in enumerate((vals_ref[1, band], prec_ref[1, band], vals_ref[0, band])):
+            moved = pltpu.roll(spare, turns[place], 1)
+            both = jnp.where(lane < channels, filled(part), moved)
+            if place < 2:
+                late_ref[band, :, place * LANES : (place + 1) * LANES] = both.astype(bf16)
+            else:
+                early_ref[band] = both.astype(bf16)
         return carry
 
     lax.fori_loop(0, count, obs_row, 0)
@@ -226,27 +236,36 @@
 
     pl.semaphore_wait(barrier, count - 1)
 
-    def send(ref, at):
-        for copy in halo_copies(ref, sems, at):
+    strip = REACH * lat_cols
+    total_rows = lon_rows * lat_cols
+
+    def send(at, west, east):
+        edge_ref[at, 0] = west.astype(bf16)
+        edge_ref[at, 1] = east.astype(bf16)
+        for copy in edge_copies(edge_ref, halo_ref, sems, at):
             copy.start()
 
-    def arrive(ref, at):
-        for copy in halo_copies(ref, sems, at):
+    def send_state(at):
+        send(at, one_ref[0:strip, :], one_ref[total_rows - strip :, :])
+
+    def arrive(at):
+        for copy in edge_copies(edge_ref, halo_ref, sems, at):
             copy.wait()
 
-        def ends(k, carry):
-            row = jnp.where(k < REACH, k, lon_rows + k)
-            low = ref[row, REACH : 2 * REACH].astype(f32)
-            high = ref[row, runs : runs + REACH].astype(f32)
-            put_ends(ref, row, low, high)
-            return carry
-
-        lax.fori_loop(0, 2 * REACH, ends, 0)
+    def arrive_state(at, xp_ref):
+        arrive(at)
+        for side, first in enumerate((-REACH, lon_rows)):
+            lifted = jnp.dot(halo_ref[at, side], liftp_ref[...], preferred_element_type=f32)
+            for k in range(REACH):
+                put_tiles(xp_ref, first + k, lifted[k * lat_cols : (k + 1) * lat_cols])
+
+    boxes = ((early_ref, early_in_ref), (late_ref, late_in_ref))
 
     def obs_copy(moment, step, band):
+        out_box, in_box = boxes[moment]
         return pltpu.make_async_remote_copy(
-            src_ref=sb_ref.at[moment, band],
-            dst_ref=rb_ref.at[moment, here],
+            src_ref=out_box.at[band],
+            dst_ref=in_box.at[here],
             send_sem=obs_send.at[moment, step - 1],
             recv_sem=obs_recv.at[moment, step - 1],
             device_id={"lon": peer(step)},
@@ -254,9 +273,8 @@
         )
 
     def own_copy(moment):
-        return pltpu.make_async_copy(
-            sb_ref.at[moment, here], rb_ref.at[moment, here], own_sem.at[moment]
-        )
+        out_box, in_box = boxes[moment]
+        return pltpu.make_async_copy(out_box.at[here], in_box.at[here], own_sem.at[moment])
 
     def obs_start(moment):
         def start(step, carry):
@@ -270,9 +288,10 @@
         def wait(step, carry):
             obs_copy(moment, step, peer(step)).wait_send()
             source = peer(count - step)
+            out_box, in_box = boxes[moment]
             pltpu.make_async_remote_copy(
-                src_ref=sb_ref.at[moment, source],
-                dst_ref=rb_ref.at[moment, source],
+                src_ref=out_box.at[source],
+                dst_ref=in_box.at[source],
                 send_sem=obs_send.at[moment, step - 1],
                 recv_sem=obs_recv.at[moment, step - 1],
                 device_id={"lon": peer(step)},
@@ -324,7 +343,7 @@
 
     def conv_inner(xp_ref, flip):
         def body(o, carry):
-            conv_row(xp_ref, kb_ref, mix_ref, o, flip)
+            conv_row(xp_ref, kb_ref, mix_ref, o, o, flip)
             return carry
 
         lax.fori_loop(REACH, lon_rows - REACH, body, 0)
@@ -332,10 +351,24 @@
     def conv_outer(xp_ref, flip):
         def body(k, carry):
             o = jnp.where(k < REACH, k, lon_rows - 2 * REACH + k)
-            conv_row(xp_ref, kb_ref, mix_ref, o, flip)
+            conv_row(xp_ref, kb_ref, mix_ref, o, o, flip)
             return carry
 
         lax.fori_loop(0, 2 * REACH, body, 0)
+
+    def conv_own(xp_ref):
+        for k in range(REACH):
+            conv_row(xp_ref, kb_ref, mix_ref, k, k, True, range(REACH - k, TAPS))
+            o = lon_rows - 1 - k
+            conv_row(xp_ref, kb_ref, mix_ref, o, o, True, range(0, TAPS - REACH + k))
+
+    def send_landing(at, xp_ref):
+        for k in range(REACH):
+            conv_row(xp_ref, kb_ref, land_ref, k - REACH, k, True, range(2 * REACH - k, TAPS))
+            conv_row(xp_ref, kb_ref, land_ref, lon_rows + k, REACH + k, True, range(0, REACH - k))
+        landed = land_ref[...].reshape(2 * strip, hidden).astype(bf16)
+        g_state = lax.dot_general(landed, liftp_ref[...], ACROSS, preferred_element_type=f32)
+        send(at, g_state[:strip], g_state[strip:])
 
     def forward(step, part, xp_ref, source_ref, target_ref, next_ref):
         mixed = sums(part)
@@ -392,35 +425,61 @@
         lines = jnp.zeros((spots, slots), f32)
         for p in range(points):
             hit = spot[p : p + 1, :] == number
-            lines = lines + jnp.where(hit, weight[p : p + 1, :], 0.0)
-        op_ref[...] = lines.T.astype(bf16)
+            lines = jnp.where(hit, lines + weight[p : p + 1, :], lines)
+        op_ref[moment] = lines.T.astype(bf16)
         places = count * cap
         code = code_ref[moment]
         line = lax.broadcasted_iota(jnp.int32, (slots, LANES), 1).astype(f32)
         select = jnp.concatenate(
             [
-                jnp.where(line + float(start) == code, 1.0, 0.0).astype(bf16)
+                jnp.where(code - float(start) == line, 1.0, 0.0).astype(bf16)
                 for start in range(0, places, LANES)
             ],
             axis=1,
         )
-        data = rb_ref[moment].reshape(places, 2 * LANES)
-        chosen_ref[...] = jnp.dot(select, data, preferred_element_type=f32)
+        data = late_in_ref[...].reshape(places, 2 * LANES)
+        chosen = jnp.dot(select, data, preferred_element_type=f32)
+        if moment == 0:
+            data = early_in_ref[...].reshape(places, LANES)
+            third = jnp.dot(select, data, preferred_element_type=f32)
+            tiles3 = (chosen[:, :LANES], chosen[:, LANES:], third)
+            back = [pltpu.roll(t, (LANES - n) % LANES, 1) for t, n in zip(tiles3, turns)]
+            lane = lax.broadcasted_iota(jnp.int32, (slots, LANES), 1)
+            start = channels - 2 * free
+            weights = jnp.where(
+                lane < start, back[2], jnp.where(lane < start + free, back[0], back[1])
+            )
+            weights = jnp.where(lane < channels, weights, 0.0)
+            chosen = jnp.concatenate([third, weights], axis=1)
+        chosen_ref[moment] = chosen
         size = slots // BLOCKS
         for block in range(BLOCKS):
             at = pl.ds(block, spots, stride=BLOCKS)
             mine = slice(block * size, (block + 1) * size)
-            op = op_ref[mine, :]
+            op = op_ref[moment, mine, :]
             equiv = jnp.dot(op, state_ref[at, :].astype(bf16), preferred_element_type=f32)
-            misfit = chosen_ref[mine, LANES:] * (equiv - chosen_ref[mine, :LANES])
+            chosen = chosen_ref[moment, mine, :]
+            misfit = chosen[:, LANES:] * (equiv - chosen[:, :LANES])
+            lane = lax.broadcasted_iota(jnp.int32, (size, LANES), 1)
+            misfit = jnp.where(lane < channels, misfit, 0.0)
             target_ref[at, :] = lax.dot_general(
                 op, misfit.astype(bf16), DOWN, preferred_element_type=f32
             )
 
-    def gathered(part):
+    def gathered(part, at):
         g_lifted = (take(cells(gblk_ref), part).astype(f32) + sums(part)).astype(bf16)
         g_state = lax.dot_general(g_lifted, liftp_ref[...], ACROSS, preferred_element_type=f32)
-        return take(cells(cot_ref), part) + g_state
+        value = take(cells(cot_ref), part) + g_state
+        if part != edges:
+            return value
+        return jnp.concatenate(
+            [
+                value[:strip] + halo_ref[at, 0].astype(f32),
+                value[strip:-strip],
+                value[-strip:] + halo_ref[at, 1].astype(f32),
+            ],
+            axis=0,
+        )
 
     def backward(step, part, xp_ref, cotangent):
         g_block = jnp.dot(cotangent.astype(bf16), outp_ref[...], preferred_element_type=f32)
@@ -446,7 +505,7 @@
         put_field(xp_ref, part, g_mixed)
 
     def leave(part):
-        put(cot_ref, part, gathered(part))
+        put(cot_ref, part, gathered(part, 3))
         for a, b in part:
 
             def body(o, carry):
@@ -459,43 +518,43 @@
             lax.fori_loop(a, b, body, 0)
 
 
-    send(xp0_ref, 0)
+    send_state(0)
     obs_start(1)
     conv_inner(xp0_ref, False)
     forward(0, inner, xp0_ref, one_ref, one_ref, xp1_ref)
-    arrive(xp0_ref, 0)
+    arrive_state(0, xp0_ref)
     conv_outer(xp0_ref, False)
     forward(0, edges, xp0_ref, one_ref, one_ref, xp1_ref)
-    send(xp1_ref, 1)
+    send_state(1)
     conv_inner(xp1_ref, False)
     forward(1, inner, xp1_ref, one_ref, two_ref, None)
-    arrive(xp1_ref, 1)
+    arrive_state(1, xp1_ref)
     obs_start(0)
     conv_outer(xp1_ref, False)
     forward(1, edges, xp1_ref, one_ref, two_ref, None)
     obs_wait(1)
     observe(1, two_ref, cot_ref)
     backward(1, edges, xp2_ref, take(cells(cot_ref), edges))
-    send(xp2_ref, 2)
+    send_landing(2, xp2_ref)
     backward(1, inner, xp2_ref, take(cells(cot_ref), inner))
+    conv_own(xp2_ref)
     conv_inner(xp2_ref, True)
     obs_wait(0)
     observe(0, one_ref, pull_ref)
-    arrive(xp2_ref, 2)
-    conv_outer(xp2_ref, True)
+    arrive(2)
 
     def carried(part):
-        value = gathered(part) + take(cells(pull_ref), part)
+        value = gathered(part, 2) + take(cells(pull_ref), part)
         put(cot_ref, part, value)
         return value
 
     backward(0, edges, xp3_ref, carried(edges))
-    send(xp3_ref, 3)
+    send_landing(3, xp3_ref)
     backward(0, inner, xp3_ref, carried(inner))
+    conv_own(xp3_ref)
     conv_inner(xp3_ref, True)
     leave(inner)
-    arrive(xp3_ref, 3)
-    conv_outer(xp3_ref, True)
+    arrive(3)
     leave(edges)
 
 
@@ -544,11 +603,17 @@
             pltpu.VMEM((2, amount, LANES), f32),
             pltpu.VMEM((2, amount, wide), bf16),
             pltpu.VMEM((amount, hidden), bf16),
+            pltpu.VMEM((2 * REACH, runs, BLOCKS, hidden), f32),
+            pltpu.VMEM((4, 2, REACH * lat_cols, LANES), bf16),
+            pltpu.VMEM((4, 2, REACH * lat_cols, LANES), bf16),
             pltpu.VMEM((2, slots, LANES), f32),
-            pltpu.VMEM((slots, lon_rows * runs), bf16),
-            pltpu.VMEM((slots, 2 * LANES), f32),
-            pltpu.VMEM((2, count, cap, 2 * LANES), bf16),
-            pltpu.VMEM((2, count, cap, 2 * LANES), bf16),
+            pltpu.VMEM((2, slots, lon_rows * runs), bf16),
+            pltpu.VMEM((2, slots, 2 * LANES), f32),
+            *[
+                pltpu.VMEM((count, cap, 2 * LANES), bf16),
+                pltpu.VMEM((count, cap, LANES), bf16),
+            ]
+            * 2,
             pltpu.SemaphoreType.DMA((8,)),
             pltpu.SemaphoreType.DMA((8,)),
             pltpu.SemaphoreType.DMA((2, count - 1)),

time: 61.8 us -> 58 us (0.939); the launches traced: 60.7 us -> 57.8 us
  Pallas kernels: 58.6 us -> 55.8 us
    pallas_call x1, Pallas kernels: 58.6 us -> 55.8 us  [shards(): pl.pallas_call(whole_kernel, out_shape=jax.ShapeDtypeStruct((channels * l...]
where the time goes in v3:
time: 58 us; the launch traced here: 57.8 us
  Pallas kernels  55.8 us (96%)
  local copies, waits for them, and re-layouts  2.06 us (4%)
    pallas_call x1, Pallas kernels, shards(): pl.pallas_call(whole_kernel, out_shape=jax.ShapeDtypeStruct((channels * l...  55.8 us
    unnamed x1, local copies, waits for them, and re-layouts  2.06 us

profile of v3, /device:TPU:11, one launch (start us, length us, event | category | flops | bytes accessed | tf_op | source)
XLA Modules:
  0.0 57.8 jit_solution(13724855853433925252)
XLA Ops:
  0.0 55.8 %shard_map.127 = f32[1520,128]{1,0:T(8,128)} custom-call(f32[1520,128]{1,0:T(8,128)} %bitcast.12, bf16[95,256]{1,0:T(8,128)(2,1)} %lift_ref.1, f32[49,256]{1,0:T(8,128)} %kern_ref.1, f32[1,256]{1,0:T(1,128)} %bitcast.17, bf16[256,1024]{1,0:T(8,128)(2,1)} %up_ref.1, bf16[1024,256]{1,0:T(8,128)(2,1)} %down_ref.1, bf16[95,256]{1,0:T(8,128)(2,1)} %bitcast.15, ...), custom_call_target="tpu_custom_call" | custom-call | tf_op jit(solution)/shard_map/pallas_call | solution.py:587
  55.8 2.1 %copy.15 = f32[95,16,128]{2,1,0:T(8,128)} copy(f32[95,16,128]{2,1,0:T(8,128)} %bitcast.9) | data formatting | bytes 1556480

commit v4 on v3

--- a/solution.py
+++ b/solution.py
@@ -65,8 +65,8 @@
 def conv_row(xp_ref, kb_ref, mix_ref, o, to, flip, taps=range(TAPS)):
     runs = mix_ref.shape[1]
     last = TAPS * TAPS - 1
-    for first in range(0, len(taps), 2):
-        lines = taps[first : first + 2]
+    for first in range(0, len(taps), 3):
+        lines = taps[first : first + 3]
         weights = {}
         for i in lines:
             for j in range(TAPS):
@@ -88,16 +88,20 @@
     lift_ref,
     kern_ref,
     gain_ref,
-    up_ref,
-    down_ref,
+    up_hbm,
+    down_hbm,
     outw_ref,
     cell_ref,
     wts_ref,
     limit_ref,
     owner_ref,
+    vals_hbm,
+    prec_hbm,
+    out_ref,
+    up_ref,
+    down_ref,
     vals_ref,
     prec_ref,
-    out_ref,
     tin_ref,
     nat_ref,
     pad_ref,
@@ -117,6 +121,7 @@
     inverse_ref,
     slope_ref,
     gblk_ref,
+    mid_ref,
     land_ref,
     edge_ref,
     halo_ref,
@@ -132,6 +137,7 @@
     obs_send,
     obs_recv,
     own_sem,
+    load_sem,
 ):
     count = lax.axis_size("lon")
     here = lax.axis_index("lon")
@@ -159,6 +165,19 @@
         return carry
 
     lax.fori_loop(1, count, greet, 0)
+    loads = [
+        pltpu.make_async_copy(source, target, load_sem.at[k])
+        for k, (source, target) in enumerate(
+            (
+                (vals_hbm, vals_ref),
+                (prec_hbm, prec_ref),
+                (up_hbm, up_ref),
+                (down_hbm, down_ref),
+            )
+        )
+    ]
+    for load in loads:
+        load.start()
 
 
     for ref, into_ref in ((lift_ref, liftp_ref), (outw_ref, outp_ref)):
@@ -189,6 +208,9 @@
 
     lax.fori_loop(0, lon_rows, enter, 0)
 
+
+    for load in loads:
+        load.wait()
 
     free = LANES - channels
     turns = [(channels - (channels - free * (2 - k))) % LANES for k in range(2)] + [channels]
@@ -485,7 +507,6 @@
         g_block = jnp.dot(cotangent.astype(bf16), outp_ref[...], preferred_element_type=f32)
         g_block = g_block.astype(bf16)
         put(gblk_ref, part, g_block)
-        total = None
         piece = 256
         for start in range(0, wide, piece):
             cut = slice(start, start + piece)
@@ -493,10 +514,8 @@
                 g_block, down_ref[cut, :], ACROSS, preferred_element_type=f32
             )
             slope = take(lambda a, b: slope_ref[step, a * lat_cols : b * lat_cols, cut], part)
-            term = lax.dot_general(
-                g_active.astype(bf16) * slope, up_ref[:, cut], ACROSS, preferred_element_type=f32
-            )
-            total = term if total is None else total + term
+            mid_ref[:, cut] = g_active.astype(bf16) * slope
+        total = lax.dot_general(mid_ref[...], up_ref[...], ACROSS, preferred_element_type=f32)
         g_scaled = total * gain_ref[...]
         normal = take(leading(normal_ref, step), part).astype(f32)
         inverse = take(leading(inverse_ref, step), part)
@@ -505,17 +524,7 @@
         put_field(xp_ref, part, g_mixed)
 
     def leave(part):
-        put(cot_ref, part, gathered(part, 3))
-        for a, b in part:
-
-            def body(o, carry):
-                base = o * lat_cols
-                rows = [cot_ref[pl.ds(base + k, runs, stride=BLOCKS), :] for k in range(BLOCKS)]
-                turned = jnp.concatenate(rows, axis=0).T
-                out_ref[pl.ds(o, channels, stride=lon_rows), :] = turned[:channels]
-                return carry
-
-            lax.fori_loop(a, b, body, 0)
+        put(out_ref, part, gathered(part, 3))
 
 
     send_state(0)
@@ -536,11 +545,11 @@
     observe(1, two_ref, cot_ref)
     backward(1, edges, xp2_ref, take(cells(cot_ref), edges))
     send_landing(2, xp2_ref)
+    obs_wait(0)
+    observe(0, one_ref, pull_ref)
     backward(1, inner, xp2_ref, take(cells(cot_ref), inner))
     conv_own(xp2_ref)
     conv_inner(xp2_ref, True)
-    obs_wait(0)
-    observe(0, one_ref, pull_ref)
     arrive(2)
 
     def carried(part):
@@ -556,6 +565,32 @@
     leave(inner)
     arrive(3)
     leave(edges)
+
+
+def turn_kernel(cells_hbm, out_ref, cells_ref, sem):
+    lat_cols = out_ref.shape[1]
+    lon_rows = cells_ref.shape[0] // lat_cols
+    channels = out_ref.shape[0] // lon_rows
+    runs = lat_cols // BLOCKS
+    parts = sem.shape[0]
+    size = lon_rows // parts
+    loads = []
+    for k in range(parts):
+        at = pl.ds(k * size * lat_cols, size * lat_cols)
+        load = pltpu.make_async_copy(cells_hbm.at[at], cells_ref.at[at], sem.at[k])
+        load.start()
+        loads.append(load)
+
+    def body(o, carry):
+        base = o * lat_cols
+        rows = [cells_ref[pl.ds(base + k, runs, stride=BLOCKS), :] for k in range(BLOCKS)]
+        turned = jnp.concatenate(rows, axis=0).T
+        out_ref[pl.ds(o, channels, stride=lon_rows), :] = turned[:channels]
+        return carry
+
+    for k, load in enumerate(loads):
+        load.wait()
+        lax.fori_loop(k * size, (k + 1) * size, body, 0, unroll=2)
 
 
 def shards(
@@ -583,13 +618,17 @@
 
     vmem = pl.BlockSpec(memory_space=pltpu.VMEM)
     smem = pl.BlockSpec(memory_space=pltpu.SMEM)
+    hbm = pl.BlockSpec(memory_space=pl.ANY)
     field = (lon_rows + 2 * REACH, runs + 2 * REACH, BLOCKS, hidden)
     result = pl.pallas_call(
         whole_kernel,
-        out_shape=jax.ShapeDtypeStruct((channels * lon_rows, lat_cols), f32),
-        in_specs=[vmem] * 9 + [smem] + [vmem] * 3,
+        out_shape=jax.ShapeDtypeStruct((amount, LANES), f32),
+        in_specs=[vmem] * 4 + [hbm] * 2 + [vmem] * 3 + [smem, vmem] + [hbm] * 2,
         out_specs=vmem,
         scratch_shapes=[
+            pltpu.VMEM((hidden, wide), bf16),
+            pltpu.VMEM((wide, hidden), bf16),
+            *[pltpu.VMEM((2, count, cap, channels), f32)] * 2,
             pltpu.VMEM((LANES, LANES), f32),
             pltpu.VMEM((LANES, LANES), f32),
             pltpu.VMEM((LANES, hidden), f32),
@@ -603,6 +642,7 @@
             pltpu.VMEM((2, amount, LANES), f32),
             pltpu.VMEM((2, amount, wide), bf16),
             pltpu.VMEM((amount, hidden), bf16),
+            pltpu.VMEM((amount // 2, wide), bf16),
             pltpu.VMEM((2 * REACH, runs, BLOCKS, hidden), f32),
             pltpu.VMEM((4, 2, REACH * lat_cols, LANES), bf16),
             pltpu.VMEM((4, 2, REACH * lat_cols, LANES), bf16),
@@ -619,6 +659,7 @@
             pltpu.SemaphoreType.DMA((2, count - 1)),
             pltpu.SemaphoreType.DMA((2, count - 1)),
             pltpu.SemaphoreType.DMA((2,)),
+            pltpu.SemaphoreType.DMA((4,)),
         ],
         compiler_params=pltpu.CompilerParams(
             vmem_limit_bytes=VMEM_LIMIT, collective_id=0, has_side_effects=True
@@ -638,7 +679,15 @@
         obs_values[:, 0],
         obs_precision[:, 0],
     )
-    return result.reshape(channels, lon_rows, lat_cols)
+    turned = pl.pallas_call(
+        turn_kernel,
+        out_shape=jax.ShapeDtypeStruct((channels * lon_rows, lat_cols), f32),
+        in_specs=[hbm],
+        out_specs=vmem,
+        scratch_shapes=[pltpu.VMEM((amount, LANES), f32), pltpu.SemaphoreType.DMA((4,))],
+        compiler_params=pltpu.CompilerParams(vmem_limit_bytes=VMEM_LIMIT),
+    )(result)
+    return turned.reshape(channels, lon_rows, lat_cols)
 
 
 def solution(mesh):

time: 58 us -> 56.7 us (0.978)
  local copies, waits for them, and re-layouts: 2.06 us -> 0 us
  Pallas kernels: 55.8 us -> 56.4 us
    unnamed x1 -> x0, local copies, waits for them, and re-layouts: 2.06 us -> none
    pallas_call x1 -> x2, Pallas kernels: 55.8 us -> 56.4 us  [the longest x1 53.7 us: shards(): pl.pallas_call(whole_kernel, out_shape=jax.ShapeDtypeStruct((amount, LANE...]
where the time goes in v4:
time: 56.7 us; the launch traced here: 56.6 us
  Pallas kernels  56.4 us (99%)
    pallas_call x1, Pallas kernels, shards(): pl.pallas_call(whole_kernel, out_shape=jax.ShapeDtypeStruct((amount, LANE...  53.7 us
    pallas_call x1, Pallas kernels, shards(): pl.pallas_call(turn_kernel, out_shape=jax.ShapeDtypeStruct((channels * lo...  2.66 us

profile of v4, /device:TPU:11, one launch (start us, length us, event | category | flops | bytes accessed | tf_op | source)
XLA Modules:
  0.0 56.6 jit_solution(12684152534790667038)
XLA Ops:
  0.0 53.7 %shard_map.127.cells_hbm = f32[2048,128]{1,0:T(8,128)} custom-call(f32[1520,128]{1,0:T(8,128)} %bitcast.11, bf16[95,256]{1,0:T(8,128)(2,1)} %lift_ref.1, f32[49,256]{1,0:T(8,128)} %kern_ref.1, f32[1,256]{1,0:T(1,128)} %bitcast.16, bf16[256,1024]{1,0:T(8,128)(2,1)} %up_hbm.1, bf16[1024,256]{1,0:T(8,128)(2,1)} %down_hbm.1, bf16[95,256]{1,0:T(8,128)(2,1)} %bitcast.14, ...), custom_call_target="tpu_custom_call" | custom-call | tf_op jit(solution)/shard_map/pallas_call | solution.py:623
  53.7 2.7 %shard_map.128 = f32[1520,128]{1,0:T(8,128)} custom-call(f32[2048,128]{1,0:T(8,128)} %shard_map.127.cells_hbm), custom_call_target="tpu_custom_call" | custom-call | tf_op jit(solution)/shard_map/pallas_call | solution.py:682

commit v5 on v4

--- a/solution.py
+++ b/solution.py
@@ -545,11 +545,11 @@
     observe(1, two_ref, cot_ref)
     backward(1, edges, xp2_ref, take(cells(cot_ref), edges))
     send_landing(2, xp2_ref)
-    obs_wait(0)
-    observe(0, one_ref, pull_ref)
     backward(1, inner, xp2_ref, take(cells(cot_ref), inner))
     conv_own(xp2_ref)
     conv_inner(xp2_ref, True)
+    obs_wait(0)
+    observe(0, one_ref, pull_ref)
     arrive(2)
 
     def carried(part):

time: 56.7 us -> 57.3 us (1.011)
  Pallas kernels: 56.4 us -> 57 us
    pallas_call x1, Pallas kernels: 53.7 us -> 54.3 us  [shards(): pl.pallas_call(whole_kernel, out_shape=jax.ShapeDtypeStruct((amount, LANE...]
where the time goes in v5:
time: 57.3 us; the launch traced here: 57.2 us
  Pallas kernels  57 us (99%)
    pallas_call x1, Pallas kernels, shards(): pl.pallas_call(whole_kernel, out_shape=jax.ShapeDtypeStruct((amount, LANE...  54.3 us
    pallas_call x1, Pallas kernels, shards(): pl.pallas_call(turn_kernel, out_shape=jax.ShapeDtypeStruct((channels * lo...  2.66 us

profile of v5, /device:TPU:11, one launch (start us, length us, event | category | flops | bytes accessed | tf_op | source)
XLA Modules:
  0.0 57.2 jit_solution(3959746776111528903)
XLA Ops:
  0.0 54.3 %shard_map.127.cells_hbm = f32[2048,128]{1,0:T(8,128)} custom-call(f32[1520,128]{1,0:T(8,128)} %bitcast.11, bf16[95,256]{1,0:T(8,128)(2,1)} %lift_ref.1, f32[49,256]{1,0:T(8,128)} %kern_ref.1, f32[1,256]{1,0:T(1,128)} %bitcast.16, bf16[256,1024]{1,0:T(8,128)(2,1)} %up_hbm.1, bf16[1024,256]{1,0:T(8,128)(2,1)} %down_hbm.1, bf16[95,256]{1,0:T(8,128)(2,1)} %bitcast.14, ...), custom_call_target="tpu_custom_call" | custom-call | tf_op jit(solution)/shard_map/pallas_call | solution.py:623
  54.3 2.7 %shard_map.128 = f32[1520,128]{1,0:T(8,128)} custom-call(f32[2048,128]{1,0:T(8,128)} %shard_map.127.cells_hbm), custom_call_target="tpu_custom_call" | custom-call | tf_op jit(solution)/shard_map/pallas_call | solution.py:682
